TPU v7x, 512 devices: a whole 4x4x16 slice. The times are simulated.
512 devices in a mesh: lat: 64 (over x, y, z_hi, core), lon: 8 (over z_lo).
Axes of the slice: x: 4, y: 4, z: 16 (z_hi: 2, z_lo: 8; z = z_hi * 8 + z_lo), core: 2. Of those that a mesh axis runs over, the one named last changes fastest.
Arguments:
- field: bfloat16 [128, 1440, 384], P('lat', 'lon'), may hold values from -6 to 6
- row_shift: int32 [128], P('lat'), may hold values from -1 to 1
- output_tile_index: int32 [128], P('lat'), may hold values from 0 to 15
- tiles: bfloat16 [3, 16, 3, 33], replicated, may hold values from -0.625 to 0.625
- mix: bfloat16 [3, 4, 96, 96], replicated, may hold values from -0.375 to 0.375
- w_in: bfloat16 [384, 768], replicated, may hold values from -0.3125 to 0.3125
- w_out: bfloat16 [768, 384], replicated, may hold values from -0.21875 to 0.21875
- cotangent: bfloat16 [128, 1440, 384], P('lat', 'lon'), may hold values from -6 to 6
Outputs:
- output: bfloat16 [128, 1440, 384], P('lat', 'lon')
- grad_field: bfloat16 [128, 1440, 384], P('lat', 'lon')
- grad_mix: bfloat16 [3, 4, 96, 96], replicated
- grad_in: bfloat16 [384, 768], replicated
- grad_out: bfloat16 [768, 384], replicated
All inputs are finite; a program needn't handle non-finite values.
Results may differ from a plain program's by a relative error of at most 0.0069.
Values may be sent and summed in bfloat16 or wider, within the bound.
A program may use at most 64 MiB of HBM per device.

v0:
```python
import jax
import jax.numpy as jnp
from jax import lax
from jax.sharding import PartitionSpec as P

D = 384
G = 4
DG = 96
K = 3
HB = 1
REACH = 2
WH = 16
WTAP = 33


def extended_2(value, sides, width, wrap):
    for axis, dim in sides:
        size, length = (lax.axis_size(axis), value.shape[dim])
        up = [(i, (i + 1) % size) for i in range(size if wrap else size - 1)]
        down = [(j, i) for i, j in up]
        last = lax.slice_in_dim(value, length - width, length, axis=dim)
        leading = lax.slice_in_dim(value, 0, width, axis=dim)
        before = lax.ppermute(last, axis, up)
        after = lax.ppermute(leading, axis, down)
        value = jnp.concatenate([before, value, after], axis=dim)
    return value


def body(field, row_shift, output_tile_index, tiles, mix, w_in, w_out, cotangent):
    rows_here = field.shape[0]
    lon_here = field.shape[1]
    width = lon_here + 2 * WH
    strip_row_extent = 2 * HB + 1
    extended = extended_2(field, (("lat", 0),), REACH, False)
    extended = extended_2(extended, (("lon", 1),), WH, True)
    row_index = (
        jnp.arange(rows_here, dtype=jnp.int32)[:, None]
        + row_shift[:, None]
        + jnp.arange(strip_row_extent, dtype=jnp.int32)[None, :]
        - HB
        + REACH
    )
    band_rows = extended[row_index]
    tile_onehot = (
        output_tile_index[:, None] == jnp.arange(tiles.shape[1], dtype=jnp.int32)[None, :]
    ).astype(jnp.bfloat16)
    kernel_row_offsets = jnp.einsum(
        "rn,bnkm->rbkm", tile_onehot, tiles, preferred_element_type=jnp.float32
    ).astype(jnp.bfloat16)
    offset = (
        jnp.arange(width, dtype=jnp.int32)[None, :] - jnp.arange(lon_here, dtype=jnp.int32)[:, None]
    )
    position_matrix = (
        offset[:, :, None] == jnp.arange(WTAP, dtype=jnp.int32)[None, None, :]
    ).astype(jnp.bfloat16)
    strip_layout = jnp.einsum(
        "tzsa,iwa->tzsiw", kernel_row_offsets, position_matrix, preferred_element_type=jnp.float32
    ).astype(jnp.bfloat16)
    basis = jnp.einsum(
        "rbkjp,rkpc->rbjc", strip_layout, band_rows, preferred_element_type=jnp.float32
    ).astype(jnp.bfloat16)
    grouped = basis.reshape(rows_here, K, lon_here, G, DG)
    conv = jnp.einsum("rbjgf,bgfe->rjge", grouped, mix, preferred_element_type=jnp.float32).reshape(
        rows_here, lon_here, D
    )
    mixed = (field.astype(jnp.float32) + conv).astype(jnp.bfloat16)
    flat = mixed.reshape(-1, D)
    pre = jnp.dot(flat, w_in, preferred_element_type=jnp.float32)
    hidden = jax.nn.gelu(pre).astype(jnp.bfloat16)
    output = (
        flat.astype(jnp.float32) + jnp.dot(hidden, w_out, preferred_element_type=jnp.float32)
    ).astype(jnp.bfloat16)
    grad_flat = cotangent.reshape(-1, D)
    grad_hidden = jnp.dot(grad_flat, w_out.T, preferred_element_type=jnp.float32)
    unused, gelu_back = jax.vjp(jax.nn.gelu, pre)
    grad_pre = gelu_back(grad_hidden)[0].astype(jnp.bfloat16)
    grad_mixed = (
        grad_flat.astype(jnp.float32)
        + jnp.dot(grad_pre, w_in.T, preferred_element_type=jnp.float32)
    ).astype(jnp.bfloat16)
    input_portion = jnp.dot(flat.T, grad_pre, preferred_element_type=jnp.float32)
    part_out = jnp.dot(hidden.T, grad_flat, preferred_element_type=jnp.float32)
    grad_grouped = grad_mixed.reshape(rows_here, lon_here, G, DG)
    part_mix = jnp.einsum(
        "rbjgf,rjge->bgfe", grouped, grad_grouped, preferred_element_type=jnp.float32
    )
    filter_basis_gradient = jnp.einsum(
        "rjge,bgfe->rbjgf", grad_grouped, mix, preferred_element_type=jnp.float32
    )
    filter_basis_gradient = filter_basis_gradient.reshape(rows_here, K, lon_here, D).astype(
        jnp.bfloat16
    )
    grad_band = jnp.einsum(
        "rbkjp,rbjc->rkpc", strip_layout, filter_basis_gradient, preferred_element_type=jnp.float32
    )
    grad_ext = (
        jnp.zeros((rows_here + 2 * REACH, width, D), jnp.float32).at[row_index].add(grad_band)
    )
    sides = jnp.concatenate([grad_ext[:, :WH], grad_ext[:, width - WH :]], axis=1)
    beside = extended_2(sides.astype(jnp.bfloat16), (("lon", 1),), WH, True).astype(sides.dtype)
    core = grad_ext[:, WH : WH + lon_here]
    core = core.at[:, :WH].add(beside[:, :WH])
    core = core.at[:, lon_here - WH :].add(beside[:, 3 * WH :])
    rims = jnp.concatenate([core[:REACH], core[rows_here + REACH :]], axis=0)
    above = extended_2(rims, (("lat", 0),), REACH, False)
    inner = core[REACH : REACH + rows_here]
    inner = inner.at[:REACH].add(above[:REACH])
    inner = inner.at[rows_here - REACH :].add(above[3 * REACH :])
    grad_field = (grad_mixed.astype(jnp.float32).reshape(rows_here, lon_here, D) + inner).astype(
        jnp.bfloat16
    )
    total_mix, total_in, output_total_count = lax.psum(
        (part_mix, input_portion, part_out), ("lat", "lon")
    )
    grad_mix = total_mix.astype(jnp.bfloat16)
    grad_in = total_in.astype(jnp.bfloat16)
    grad_out = output_total_count.astype(jnp.bfloat16)
    return (output.reshape(rows_here, lon_here, D), grad_field, grad_mix, grad_in, grad_out)


def solution(mesh):
    return jax.shard_map(
        body,
        mesh=mesh,
        in_specs=(
            P("lat", "lon", None),
            P("lat"),
            P("lat"),
            P(),
            P(),
            P(),
            P(),
            P("lat", "lon", None),
        ),
        out_specs=(P("lat", "lon", None), P("lat", "lon", None), P(), P(), P()),
        check_vma=False,
    )
```

profile of v0, /device:TPU:1, one launch (start us, length us, event | category | flops | bytes accessed | tf_op | source)
XLA Modules:
  0.0 314.6 jit_solution(13332935188188742552)
XLA Ops:
  0.6 1.1 copy.69
  1.7 16.8 %collective-permute-start = (bf16[2,180,384]{2,1,0:T(8,128)(2,1)S(1)}, bf16[2,180,384]{2,1,0:T(8,128)(2,1)S(1)}, u32[]{:S(2)}, u32[]{:S(2)}) collective-permute-start(bf16[2,180,384]{2,1,0:T(8,128)(2,1)S(1)} %copy.69), channel_id=1, source_target_pairs={{0,8},{8,16},{16,24},{24,32},{32,40},{40,48},{48,56},{56,64},{64,7... | collective-permute-start | bytes 829448 | tf_op jit(solution)/shard_map/ppermute | solution.py:23
  18.5 1.9 collective-permute-start.1
  20.5 0.7 iota_add_fusion
  21.2 4.2 %fusion.4 = bf16[2,3,3,180,212]{4,0,3,2,1:T(2,128)(2,1)} fusion(s32[180,212]{1,0:T(8,128)S(1)} %iota_subtract_fusion, bf16[3,16,3,33]{3,1,2,0:T(8,128)(2,1)} %param.23, s32[2]{0:T(128)} %param.22), kind=kOutput, calls=%fused_computation.6 | convolution fusion | flops 47299872 | bytes 1535912 | tf_op jit(solution)/shard_map/tzsa,iwa->tzsiw/dot_general | solution.py:56
  25.4 0.1 compare_select_fusion
  25.5 0.1 reshape.230
  25.6 0.1 reshape.222
  25.7 0.8 copy-done.10
  26.5 1.5 fusion.47
  28.0 8.3 %collective-permute-done = bf16[2,180,384]{2,1,0:T(8,128)(2,1)S(1)} collective-permute-done((bf16[2,180,384]{2,1,0:T(8,128)(2,1)S(1)}, bf16[2,180,384]{2,1,0:T(8,128)(2,1)S(1)}, u32[]{:S(2)}, u32[]{:S(2)}) %collective-permute-start) | collective-permute-done | bytes 276512 | tf_op jit(solution)/shard_map/ppermute | solution.py:23
  36.2 0.1 constant_dynamic-update-slice_fusion.1
  36.3 4.0 %collective-permute-done.1 = bf16[2,180,384]{2,1,0:T(8,128)(2,1)S(1)} collective-permute-done((bf16[2,180,384]{2,1,0:T(8,128)(2,1)S(1)}, bf16[2,180,384]{2,1,0:T(8,128)(2,1)S(1)}, u32[]{:S(2)}, u32[]{:S(2)}) %collective-permute-start.1) | collective-permute-done | bytes 276512 | tf_op jit(solution)/shard_map/ppermute | solution.py:24
  40.4 7.8 %collective-permute-start.2 = (bf16[6,16,384]{2,1,0:T(8,128)(2,1)S(1)}, bf16[6,16,384]{2,1,0:T(8,128)(2,1)S(1)}, u32[]{:S(2)}, u32[]{:S(2)}) collective-permute-start(bf16[6,16,384]{2,1,0:T(8,128)(2,1)S(1)} %get-tuple-element.96), channel_id=1, source_target_pairs={{0,1},{1,2},{2,3},{3,4},{4,5},{5,6},{6,7},{7,0},{8,9},{9,10},{10,1... | collective-permute-start | bytes 221192 | tf_op jit(solution)/shard_map/ppermute | solution.py:23
  48.2 4.3 %collective-permute-start.3 = (bf16[6,16,384]{2,1,0:T(8,128)(2,1)S(1)}, bf16[6,16,384]{2,1,0:T(8,128)(2,1)S(1)}, u32[]{:S(2)}, u32[]{:S(2)}) collective-permute-start(bf16[6,16,384]{2,1,0:T(8,128)(2,1)S(1)} %get-tuple-element.97), channel_id=1, source_target_pairs={{1,0},{2,1},{3,2},{4,3},{5,4},{6,5},{7,6},{0,7},{9,8},{10,9},{11,1... | collective-permute-start | bytes 221192 | tf_op jit(solution)/shard_map/ppermute | solution.py:24
  52.5 1.2 collective-permute-done.3
  53.7 0.1 pad_maximum_fusion
  53.8 0.8 gather_fusion
  54.7 2.5 bitcast_convert_fusion
  57.2 0.7 reshape.218
  57.9 0.3 copy-done.12
  58.2 0.6 convolution_bitcast_fusion
  58.8 0.4 copy-done.1
  59.2 0.3 copy.78
  59.5 0.4 reshape.219
  59.9 0.1 add_convert_fusion
  59.9 0.1 reshape.220
  60.0 1.1 copy-done.9
  61.1 0.9 fusion.25
  62.1 0.5 fusion.15
  62.5 0.3 copy-done.5
  62.9 0.4 copy-done.17
  63.2 1.7 fusion.43
  64.9 0.2 reshape.225
  65.2 0.5 fusion.13
  65.7 0.4 copy.82
  66.1 0.9 reshape.255
  67.0 4.0 %fusion.7 = f32[2,3,212,384,1]{3,2,4,1,0:T(8,128)} fusion(bf16[2,3,3,180,212]{4,0,3,2,1:T(2,128)(2,1)} %fusion.4, bf16[2,3,180,384,1]{3,2,1,0,4:T(8,128)(2,1)S(1)} %reshape.255), kind=kOutput, calls=%fused_computation.8 | convolution fusion | flops 527523840 | bytes 4156992 | tf_op jit(solution)/shard_map/rbkjp,rbjc->rkpc/dot_general | solution.py:93
  71.1 0.1 broadcast_in_dim.2
  71.2 0.5 copy-done.16
  71.7 3.2 %scatter_fusion = f32[6,212,384]{2,1,0:T(8,128)S(1)} fusion(f32[6,212,384]{2,1,0:T(8,128)S(1)} %broadcast_in_dim.2, s32[6]{0:T(128)S(1)} %copy-done.16, f32[6,212,384]{2,1,0:T(8,128)} %bitcast.72), kind=kCustom, calls=%fused_computation.1 | custom fusion | flops 488448 | bytes 5861400 | tf_op jit(solution)/shard_map/scatter-add | solution.py:97
  74.9 0.1 convert.7
  75.0 0.7 fusion.45
  75.7 1.9 collective-permute-start.4
  77.6 10.3 %collective-permute-start.5 = (bf16[6,16,384]{2,1,0:T(8,128)(2,1)}, bf16[6,16,384]{2,1,0:T(8,128)(2,1)}, u32[]{:S(2)}, u32[]{:S(2)}) collective-permute-start(bf16[6,16,384]{2,1,0:T(8,128)(2,1)} %get-tuple-element.95), channel_id=1, source_target_pairs={{1,0},{2,1},{3,2},{4,3},{5,4},{6,5},{7,6},{0,7},{9,8},{10,9},{11,1... | collective-permute-start | bytes 221192 | tf_op jit(solution)/shard_map/ppermute | solution.py:24
  88.0 1.2 fusion.14
  89.2 0.9 reshape.227
  90.1 1.3 slice.137
  91.4 1.0 reshape.221
  92.4 0.9 copy.90
  93.3 1.6 fusion.34
  94.9 1.0 slice_add_fusion.1
  95.9 1.7 scatter-add.16
  97.6 1.3 fusion.44
  98.9 1.1 copy.84
  100.0 1.1 copy.86
  101.1 2.0 collective-permute-start.7
  103.2 12.6 %collective-permute-start.6 = (f32[2,180,384]{2,0,1:T(2,128)}, f32[2,180,384]{2,0,1:T(2,128)}, u32[]{:S(2)}, u32[]{:S(2)}) collective-permute-start(f32[2,180,384]{2,0,1:T(2,128)} %copy.84), channel_id=1, source_target_pairs={{0,8},{8,16},{16,24},{24,32},{32,40},{40,48},{48,56},{56,64},{64,7... | collective-permute-start | bytes 1658888 | tf_op jit(solution)/shard_map/ppermute | solution.py:23
  115.8 0.5 fusion.48
  116.3 0.4 convolution_bitcast_fusion.1
  116.7 193.7 %all-reduce.2 = (bf16[3,4,96,96]{2,3,0,1:T(8,128)(2,1)}, bf16[384,768]{1,0:T(8,128)(2,1)}, bf16[768,384]{1,0:T(8,128)(2,1)}) all-reduce(f32[3,4,96,96]{2,3,0,1:T(8,128)S(1)} %convolution_bitcast_fusion.1, f32[384,768]{1,0:T(8,128)S(1)} %fusion.48, f32[768,384]{1,0:T(8,128)} %fusion.43), channel_id=1, replica_groups=mesh['lat'=64,'lon'=8] {'lat','lon'}, use_global_device_ids=true, to_apply=%region_1.0 | all-reduce | flops 700416 | bytes 4202496 | tf_op jit(solution)/shard_map/psum | solution.py:112
  310.4 1.8 copy.92
  312.3 1.4 fusion.29
  313.6 0.9 copy.91
  (42 shorter events, 0.2 us)
Async XLA Ops:
  0.6 59.4 %copy-start = (bf16[384,768]{1,0:T(8,128)(2,1)S(1)}, bf16[384,768]{1,0:T(8,128)(2,1)}, u32[]{:S(2)}) copy-start(bf16[384,768]{1,0:T(8,128)(2,1)} %param.25) | copy-start | bytes 1769476
  1.7 34.5 %collective-permute-start = (bf16[2,180,384]{2,1,0:T(8,128)(2,1)S(1)}, bf16[2,180,384]{2,1,0:T(8,128)(2,1)S(1)}, u32[]{:S(2)}, u32[]{:S(2)}) collective-permute-start(bf16[2,180,384]{2,1,0:T(8,128)(2,1)S(1)} %copy.69), channel_id=1, source_target_pairs={{0,8},{8,16},{16,24},{24,32},{32,40},{40,48},{48,56},{56,64},{64,7... | collective-permute-start | bytes 829448 | tf_op jit(solution)/shard_map/ppermute | solution.py:23
  18.5 21.8 %collective-permute-start.1 = (bf16[2,180,384]{2,1,0:T(8,128)(2,1)S(1)}, bf16[2,180,384]{2,1,0:T(8,128)(2,1)S(1)}, u32[]{:S(2)}, u32[]{:S(2)}) collective-permute-start(bf16[2,180,384]{2,1,0:T(8,128)(2,1)S(1)} %copy.69), channel_id=1, source_target_pairs={{8,0},{16,8},{24,16},{32,24},{40,32},{48,40},{56,48},{64,56},{72,6... | collective-permute-start | bytes 829448 | tf_op jit(solution)/shard_map/ppermute | solution.py:24
  21.2 4.4 %copy-start.14 = (bf16[2,180,384]{2,0,1:T(2,128)(2,1)S(1)}, bf16[2,180,384]{2,0,1:T(2,128)(2,1)}, u32[]{:S(2)}) copy-start(bf16[2,180,384]{2,0,1:T(2,128)(2,1)} %param.27) | copy-start | bytes 829444
  25.4 1.1 copy-start.10
  25.6 27.0 %copy-start.15 = (s32[6]{0:T(128)}, s32[6]{0:T(128)S(1)}, u32[]{:S(2)}) copy-start(s32[6]{0:T(128)S(1)} %reshape.230) | copy-start | bytes 76
  26.5 9.8 %copy-start.3 = (bf16[2,180,384]{2,0,1:T(2,128)(2,1)S(1)}, bf16[2,180,384]{2,0,1:T(2,128)(2,1)}, u32[]{:S(2)}) copy-start(bf16[2,180,384]{2,0,1:T(2,128)(2,1)} %param.20) | copy-start | bytes 829444
  40.4 12.1 %collective-permute-start.2 = (bf16[6,16,384]{2,1,0:T(8,128)(2,1)S(1)}, bf16[6,16,384]{2,1,0:T(8,128)(2,1)S(1)}, u32[]{:S(2)}, u32[]{:S(2)}) collective-permute-start(bf16[6,16,384]{2,1,0:T(8,128)(2,1)S(1)} %get-tuple-element.96), channel_id=1, source_target_pairs={{0,1},{1,2},{2,3},{3,4},{4,5},{5,6},{6,7},{7,0},{8,9},{9,10},{10,1... | collective-permute-start | bytes 221192 | tf_op jit(solution)/shard_map/ppermute | solution.py:23
  48.2 5.5 %collective-permute-start.3 = (bf16[6,16,384]{2,1,0:T(8,128)(2,1)S(1)}, bf16[6,16,384]{2,1,0:T(8,128)(2,1)S(1)}, u32[]{:S(2)}, u32[]{:S(2)}) collective-permute-start(bf16[6,16,384]{2,1,0:T(8,128)(2,1)S(1)} %get-tuple-element.97), channel_id=1, source_target_pairs={{1,0},{2,1},{3,2},{4,3},{5,4},{6,5},{7,6},{0,7},{9,8},{10,9},{11,1... | collective-permute-start | bytes 221192 | tf_op jit(solution)/shard_map/ppermute | solution.py:24
  57.2 1.0 copy-start.12
  58.2 1.0 copy-start.1
  59.9 1.2 copy-start.9
  61.1 26.8 %copy-start.7 = (bf16[360,384]{1,0:T(8,128)(2,1)}, bf16[360,384]{1,0:T(8,128)(2,1)S(1)}, u32[]{:S(2)}) copy-start(bf16[360,384]{1,0:T(8,128)(2,1)S(1)} %reshape.220) | copy-start | bytes 829444
  62.0 0.8 copy-start.5
  62.1 1.2 copy-start.17
  63.2 1.9 copy-start.13
  71.1 0.7 copy-start.16
  74.9 13.1 %copy-start.11 = (bf16[768,384]{1,0:T(8,128)(2,1)S(1)}, bf16[768,384]{1,0:T(8,128)(2,1)}, u32[]{:S(2)}) copy-start(bf16[768,384]{1,0:T(8,128)(2,1)} %param.26) | copy-start | bytes 1769476
  74.9 13.1 %copy-start.18 = (f32[360,768]{1,0:T(8,128)S(1)}, f32[360,768]{1,0:T(8,128)}, u32[]{:S(2)}) copy-start(f32[360,768]{1,0:T(8,128)} %copy-done.17) | copy-start | bytes 3317764
  75.7 17.6 %collective-permute-start.4 = (bf16[6,16,384]{2,1,0:T(8,128)(2,1)}, bf16[6,16,384]{2,1,0:T(8,128)(2,1)}, u32[]{:S(2)}, u32[]{:S(2)}) collective-permute-start(bf16[6,16,384]{2,1,0:T(8,128)(2,1)} %get-tuple-element.94), channel_id=1, source_target_pairs={{0,1},{1,2},{2,3},{3,4},{4,5},{5,6},{6,7},{7,0},{8,9},{9,10},{10,1... | collective-permute-start | bytes 221192 | tf_op jit(solution)/shard_map/ppermute | solution.py:23
  77.6 15.7 %collective-permute-start.5 = (bf16[6,16,384]{2,1,0:T(8,128)(2,1)}, bf16[6,16,384]{2,1,0:T(8,128)(2,1)}, u32[]{:S(2)}, u32[]{:S(2)}) collective-permute-start(bf16[6,16,384]{2,1,0:T(8,128)(2,1)} %get-tuple-element.95), channel_id=1, source_target_pairs={{1,0},{2,1},{3,2},{4,3},{5,4},{6,5},{7,6},{0,7},{9,8},{10,9},{11,1... | collective-permute-start | bytes 221192 | tf_op jit(solution)/shard_map/ppermute | solution.py:24
  98.9 16.9 %copy-start.6 = (bf16[360,768]{1,0:T(8,128)(2,1)S(1)}, bf16[360,768]{1,0:T(8,128)(2,1)}, u32[]{:S(2)}) copy-start(bf16[360,768]{1,0:T(8,128)(2,1)} %copy-done.5) | copy-start | bytes 1658884
  98.9 16.9 %copy-start.8 = (bf16[360,384]{1,0:T(8,128)(2,1)S(1)}, bf16[360,384]{1,0:T(8,128)(2,1)}, u32[]{:S(2)}) copy-start(bf16[360,384]{1,0:T(8,128)(2,1)} %copy-done.7) | copy-start | bytes 829444
  101.1 15.2 %copy-start.2 = (bf16[2,3,180,4,96]{4,3,2,1,0:T(4,128)(2,1)S(1)}, bf16[2,3,180,4,96]{4,3,2,1,0:T(4,128)(2,1)}, u32[]{:S(2)}) copy-start(bf16[2,3,180,4,96]{4,3,2,1,0:T(4,128)(2,1)} %copy-done.1) | copy-start | bytes 2488324
  101.1 211.1 %collective-permute-start.7 = (f32[2,180,384]{2,0,1:T(2,128)}, f32[2,180,384]{2,0,1:T(2,128)S(1)}, u32[]{:S(2)}, u32[]{:S(2)}) collective-permute-start(f32[2,180,384]{2,0,1:T(2,128)} %copy.86), channel_id=1, source_target_pairs={{8,0},{16,8},{24,16},{32,24},{40,32},{48,40},{56,48},{64,56},{72,6... | collective-permute-start | bytes 1658888 | tf_op jit(solution)/shard_map/ppermute | solution.py:24
  103.2 209.1 %collective-permute-start.6 = (f32[2,180,384]{2,0,1:T(2,128)}, f32[2,180,384]{2,0,1:T(2,128)}, u32[]{:S(2)}, u32[]{:S(2)}) collective-permute-start(f32[2,180,384]{2,0,1:T(2,128)} %copy.84), channel_id=1, source_target_pairs={{0,8},{8,16},{16,24},{24,32},{32,40},{40,48},{48,56},{56,64},{64,7... | collective-permute-start | bytes 1658888 | tf_op jit(solution)/shard_map/ppermute | solution.py:23
  116.7 195.5 %copy-start.4 = (f32[2,180,384]{2,1,0:T(8,128)S(1)}, f32[2,180,384]{2,1,0:T(8,128)}, u32[]{:S(2)}) copy-start(f32[2,180,384]{2,1,0:T(8,128)} %reshape.227) | copy-start | bytes 1658884
where the time goes:
time: 315 us
  blocking collectives  194 us (62%)
  starting transfers between devices  57.7 us (18%)
  local copies, waits for them, and re-layouts  21.8 us (7%)
  matrix products  18.7 us (6%)
  waiting for transfers between devices  13.5 us (4%)
  other arithmetic  8.19 us (3%)
    psum x1, blocking collectives, body(): lax.psum((part_mix, input_portion, part_out), ('lat', 'lon'))  194 us
    ppermute x4, starting transfers between devices, extended_2(): before = lax.ppermute(last, axis, up)  39.1 us
    ppermute x4, starting transfers between devices, extended_2(): after = lax.ppermute(leading, axis, down)  18.6 us
    unnamed x45, local copies, waits for them, and re-layouts  8.67 us
    ppermute x4, waiting for transfers between devices, extended_2(): before = lax.ppermute(last, axis, up)  8.26 us
  transfers between devices with their start and end apart: 8, of which 3 were waited for; matrix products, arithmetic and copies ran while one was open for 5% of the time, Pallas kernels for 0%

commit v1 on v0

v1 whole, which is shorter than its diff:
```python
import functools

import jax
import jax.numpy as jnp
from jax import lax
from jax.experimental import pallas as pl
from jax.experimental.pallas import tpu as pltpu
from jax.sharding import PartitionSpec as P

D = 384
HID = 768
G = 4
DG = 96
K = 3
WTAP = 33
NLAT = 128
WH = 16
ROWS = 2
LON = 180
PAD = 192
JB = 64
NJ = 3
WIN = 128
EXT = 256
OFF = 5
CELLS = ROWS * PAD
TILES = 384
HALF = TILES // 2
PER = HALF // 16
MESH = pl.DeviceIdType.MESH
F32 = jnp.float32
BF16 = jnp.bfloat16


def dot(a, b, contract=((1,), (0,))):
    return lax.dot_general(a, b, (contract, ((), ())), preferred_element_type=F32)


def position():
    lat, lon = lax.axis_index("lat"), lax.axis_index("lon")
    return lat // 16, (lat // 4) % 4, ((lat // 2) % 2) * 8 + lon, lat % 2


def device(x, y, z, core):
    return (((x * 4 + y) * 2 + z // 8) * 2 + core, z % 8)


def remote(src, dst, send_sem, recv_sem, to):
    return pltpu.make_async_remote_copy(
        src_ref=src, dst_ref=dst, send_sem=send_sem, recv_sem=recv_sem, device_id=to, device_id_type=MESH
    )


class Halo:
    def __init__(self, sems_out, sems_in):
        lat, lon = lax.axis_index("lat"), lax.axis_index("lon")
        x, y, z, core = position()
        self.core = core
        step = 1 - 2 * core
        self.near = (lat + step, lon)
        self.far = ((lat + 64 - step) % 64, lon)
        west, east = (lon + 7) % 8, (lon + 1) % 8
        self.west, self.east = (lat, west), (lat, east)
        self.near_west, self.near_east = (lat + step, west), (lat + step, east)
        self.far_west, self.far_east = (self.far[0], west), (self.far[0], east)
        towards = 4 * (2 * core - 1)
        self.relay = device(x, y, (z + towards + 16) % 16, core)
        source_z = (z - towards + 16) % 16
        source = device(x, y, source_z, core)
        self.source = source
        self.beyond = ((source[0] + 64 - step) % 64, source[1])
        far_lat = self.far[0]
        self.passer = device(far_lat // 16, (far_lat // 4) % 4, (z + 8 - towards + 16) % 16, 1 - core)
        self.sems_out, self.sems_in = sems_out, sems_in

    def copy(self, i, src, dst, to):
        return remote(src, dst, self.sems_out.at[i], self.sems_in.at[i], to)


def kernel(
    shift_ref, index_ref, field_ref, cot_ref, tiles_ref, mix_ref, win_ref, wout_ref,
    out_ref, gfield_ref, gmix_ref, gin_ref, gout_ref,
    ext, east_in, east_out, relay, cot, taps, strip, mixd, basis, mixed, hidden, gpre, ghid, pre,
    gmixed, gbasis, gext, rim_out, rim_relay, rim_near, rim_far, side_out, side_in,
    part, core_in, half_out, plane_in, z_out, z_in, z_all, total,
    halo_s, halo_r, rim_s, rim_r, core_s, core_r, plane_s, plane_r, z_s, z_r, zg_s, zg_r, pg_s, pg_r, cg_s, cg_r,
):
    x, y, z, core = position()
    lat, lon = lax.axis_index("lat"), lax.axis_index("lon")
    halo = Halo(halo_s, halo_r)
    other = device(x, y, z, 1 - core)

    def plane_peer(k):
        px, py = (x + k // 4) % 4, (y + k % 4) % 4
        return px * 4 + py, device(px, py, z, core)

    def z_peer(k):
        pz = (z + k) % 16
        return pz, device(x, y, pz, core)

    barrier = pltpu.get_barrier_semaphore()
    greet = [halo.near, halo.far, halo.west, halo.east, halo.near_west, halo.near_east, halo.far_west, halo.far_east]
    greet += [halo.relay, halo.source, halo.beyond, halo.passer]
    greet += [plane_peer(k)[1] for k in range(1, 16)] + [z_peer(k)[1] for k in range(1, 16)]
    for to in greet:
        pl.semaphore_signal(barrier, inc=1, device_id=to, device_id_type=MESH)

    ext[2:4, PAD:EXT] = jnp.zeros((2, EXT - PAD, D), BF16)
    for r in (0, 1, 4, 5):
        ext[r, WH + PAD:EXT] = jnp.zeros((EXT - WH - PAD, D), BF16)
    for r in range(ROWS):
        ext[2 + r, WH:WH + LON] = field_ref[r]
        cot[r, PAD - 16:PAD] = jnp.zeros((16, D), BF16)
        cot[r, 0:LON] = cot_ref[r]
        edge = ext[2 + r, 176:208].astype(F32)
        east_out[r] = pltpu.roll(edge, 28, 0)[:WH].astype(BF16)

    pl.semaphore_wait(barrier, len(greet))

    near_at = core * 4
    far_at = 4 - core * 4
    sends = []
    for k in range(NJ):
        sends.append(halo.copy(k, ext.at[2:4, pl.ds(WH + JB * k, JB)], relay.at[:, pl.ds(JB * k, JB)], halo.relay))
    own_west = ext.at[2:4, 16:32]
    corners = [
        halo.copy(7, own_west, east_in.at[pl.ds(far_at, 2)], halo.far_west),
        halo.copy(8, east_out, ext.at[pl.ds(far_at, 2), 0:16], halo.far_east),
        halo.copy(9, own_west, east_in.at[2:4], halo.west),
        halo.copy(10, east_out, ext.at[2:4, 0:16], halo.east),
        halo.copy(11, own_west, east_in.at[pl.ds(near_at, 2)], halo.near_west),
        halo.copy(12, east_out, ext.at[pl.ds(near_at, 2), 0:16], halo.near_east),
    ]
    near = halo.copy(6, ext.at[2:4, WH:WH + PAD], ext.at[pl.ds(near_at, 2), WH:WH + PAD], halo.near)
    for c in sends + corners + [near]:
        c.start()

    ghid[...] = dot(cot[...].reshape(CELLS, D), wout_ref[...], ((1,), (1,)))
    group = lambda n: (n >= DG).astype(jnp.int32) + (n >= 2 * DG).astype(jnp.int32) + (n >= 3 * DG).astype(jnp.int32)
    row_i, col_i = (lax.broadcasted_iota(jnp.int32, (D, D), d) for d in (0, 1))
    block = group(row_i) == group(col_i)
    s_row, s_col = (lax.broadcasted_iota(jnp.int32, (DG, D), d) for d in (0, 1))
    spread = (s_row == s_col - DG * group(s_col)).astype(BF16)
    for b in range(K):
        wide = dot(mix_ref[b].reshape(D, DG), spread)
        mixd[D * b:D * b + D] = jnp.where(block, wide, 0.0).astype(BF16)
    taps[...] = jnp.zeros((32, 128), F32)
    for r in range(ROWS):
        s, t = shift_ref[r], index_ref[r]
        for b in range(K):
            tile = tiles_ref[b, t].astype(F32)
            for o in range(OFF):
                line = jnp.zeros((1, WTAP), F32)
                here = lat * ROWS + r + o - 2
                inside = jnp.logical_and(here >= 0, here < NLAT)
                for k in range(K):
                    line = jnp.where(jnp.logical_and(inside, k == o - 1 - s), tile[k:k + 1], line)
                n = (r * K + b) * OFF + o
                taps[n:n + 1, 0:WTAP] = line
    for r in range(ROWS):
        for b in range(K):
            for o in range(OFF):
                n = (r * K + b) * OFF + o
                line = jnp.broadcast_to(taps[n:n + 1], (JB, WIN))
                strip[r, JB * b:JB * b + JB, WIN * o:WIN * o + WIN] = pltpu.roll(
                    line, 0, 1, stride=1, stride_axis=0).astype(BF16)

    for k in range(NJ):
        sends[k].wait_recv()
        c = halo.copy(3 + k, relay.at[:, pl.ds(JB * k, JB)], ext.at[pl.ds(far_at, 2), pl.ds(WH + JB * k, JB)], halo.beyond)
        c.start()
        sends.append(c)

    near.wait_recv()
    for c in corners:
        c.wait_recv()
    for k in range(NJ):
        sends[3 + k].wait_recv()
    for c in sends[:NJ] + [near]:
        c.wait_send()
    for r in range(6):
        edge = jnp.concatenate([east_in[r].astype(F32), jnp.zeros((WH, D), F32)], axis=0)
        ext[r, PAD:PAD + 32] = (ext[r, PAD:PAD + 32].astype(F32) + pltpu.roll(edge, 4, 0)).astype(BF16)

    for r in range(ROWS):
        for j in range(NJ):
            window = ext[r:r + OFF, JB * j:JB * j + WIN].reshape(OFF * WIN, D)
            found = dot(strip[r], window).astype(BF16)
            for b in range(K):
                basis[r * PAD + JB * j:r * PAD + JB * j + JB, D * b:D * b + D] = found[JB * b:JB * b + JB]
    own = ext[2:4, WH:WH + PAD].reshape(CELLS, D).astype(F32)
    mixed[...] = (own + dot(basis[...], mixd[...])).astype(BF16)

    c0, c1 = 0.7978845608028654, 0.044715
    for n in range(3):
        pre[...] = dot(mixed[...], win_ref[:, 256 * n:256 * n + 256])

        def step(i, carry, n=n):
            at = pl.ds(pl.multiple_of(i * 64, 64), 64)
            p = pre[at, :]
            sq = p * p
            t = jnp.tanh(c0 * p * (1.0 + c1 * sq))
            half = 0.5 * (1.0 + t)
            hidden[at, 256 * n:256 * n + 256] = (p * half).astype(BF16)
            slope = half + 0.5 * p * (1.0 - t * t) * (c0 * (1.0 + 3.0 * c1 * sq))
            gpre[at, 256 * n:256 * n + 256] = (ghid[at, 256 * n:256 * n + 256] * slope).astype(BF16)
            return carry

        lax.fori_loop(0, CELLS // 64, step, 0)

    cots = cot[...].reshape(CELLS, D)
    gmixed[...] = (cots.astype(F32) + dot(gpre[...], win_ref[...], ((1,), (1,)))).astype(BF16)
    d_out = dot(hidden[...], cots, ((0,), (0,))).astype(BF16)
    for n in range(3):
        part[48 * n:48 * n + 48] = d_out[:, 128 * n:128 * n + 128].reshape(48, 16, 128)
    d_in = dot(mixed[...], gpre[...], ((0,), (0,))).astype(BF16)
    for n in range(6):
        part[144 + 24 * n:168 + 24 * n] = d_in[:, 128 * n:128 * n + 128].reshape(24, 16, 128)
    f_row, f_col = (lax.broadcasted_iota(jnp.int32, (D, 128), d) for d in (0, 1))
    fold = (f_col == f_row - DG * group(f_row)).astype(BF16)
    for b in range(K):
        d_mix = dot(basis[:, D * b:D * b + D], gmixed[...], ((0,), (0,)))
        d_mix = jnp.where(block, d_mix, 0.0).astype(BF16)
        part[288 + 24 * b:312 + 24 * b] = dot(d_mix, fold).astype(BF16).reshape(24, 16, 128)
    part[360:TILES] = jnp.zeros((TILES - 360, 16, 128), BF16)

    core_copy = remote(part.at[pl.ds(HALF * (1 - core), HALF)], core_in, core_s, core_r, other)
    core_copy.start()

    for b in range(K):
        gbasis[:, D * b:D * b + D] = dot(gmixed[...], mixd[D * b:D * b + D], ((1,), (1,))).astype(BF16)
    gext[...] = jnp.zeros((6, EXT, D), F32)
    for r in range(ROWS):
        for j in range(NJ):
            at = r * PAD + JB * j
            lines = jnp.concatenate([gbasis[at:at + JB, D * b:D * b + D] for b in range(K)], axis=0)
            piece = dot(strip[r], lines, ((0,), (0,)))
            gext[r:r + OFF, JB * j:JB * j + WIN] += piece.reshape(OFF, WIN, D)
    for r in range(6):
        rim_out[r] = gext[r, WH:WH + PAD].astype(BF16)
        side_out[0, r] = gext[r, 0:WH].astype(BF16)
        side_out[1, r] = pltpu.roll(gext[r, PAD:PAD + 32], 28, 0)[:WH].astype(BF16)
    rim = Halo(rim_s, rim_r)
    far_rows, near_rows = pl.ds(4 * core, 2), pl.ds(4 - 4 * core, 2)
    rims = []
    for k in range(NJ):
        rims.append(rim.copy(k, rim_out.at[far_rows, pl.ds(JB * k, JB)], rim_relay.at[:, pl.ds(JB * k, JB)], rim.relay))
    rim_near_copy = rim.copy(6, rim_out.at[near_rows], rim_near, rim.near)
    sides = [
        rim.copy(7, side_out.at[0, far_rows], side_in.at[0], rim.far_west),
        rim.copy(8, side_out.at[1, far_rows], side_in.at[1], rim.far_east),
        rim.copy(9, side_out.at[0, 2:4], side_in.at[2], rim.west),
        rim.copy(10, side_out.at[1, 2:4], side_in.at[3], rim.east),
        rim.copy(11, side_out.at[0, near_rows], side_in.at[4], rim.near_west),
        rim.copy(12, side_out.at[1, near_rows], side_in.at[5], rim.near_east),
    ]
    for c in rims + sides + [rim_near_copy]:
        c.start()

    core_copy.wait_recv()
    me = x * 4 + y
    plane = []
    for k in range(1, 16):
        q, to = plane_peer(k)
        mine = part[pl.ds(HALF * core + PER * q, PER)].astype(F32)
        half_out[pl.ds(PER * q, PER)] = (mine + core_in[pl.ds(PER * q, PER)].astype(F32)).astype(BF16)
        c = remote(half_out.at[pl.ds(PER * q, PER)], plane_in.at[k], plane_s.at[k], plane_r.at[k], to)
        c.start()
        plane.append(c)
    summed = part[pl.ds(HALF * core + PER * me, PER)].astype(F32) + core_in[pl.ds(PER * me, PER)].astype(F32)
    z_out[...] = summed

    out = mixed[...].astype(F32) + dot(hidden[...], wout_ref[...])
    for r in range(ROWS):
        out_ref[r] = out[r * PAD:r * PAD + LON].astype(BF16)
    for k in range(NJ):
        rims[k].wait_recv()
        c = rim.copy(3 + k, rim_relay.at[:, pl.ds(JB * k, JB)], rim_far.at[:, pl.ds(JB * k, JB)], rim.beyond)
        c.start()
        rims.append(c)

    for c in plane:
        c.wait_recv()
    for k in range(1, 16):
        z_out[...] += plane_in[k].astype(F32)
    for k in range(1, 16):
        pz, to = z_peer(k)

        @pl.when(pz % 4 != 3)
        def _(k=k, pz=pz, to=to):
            remote(z_out.at[(pz // 4) * 3 + pz % 4], z_in.at[k], z_s.at[k], z_r.at[k], to).start()

    tile = (z // 4) * 3 + jnp.minimum(z % 4, 2)
    owner = z % 4 != 3

    @pl.when(owner)
    def _():
        for k in range(1, 16):
            remote(z_out.at[0], z_in.at[k], z_s.at[k], z_r.at[k], other).wait_recv()
        acc = z_out[tile]
        for k in range(1, 16):
            acc += z_in[k]
        z_all[tile] = acc.astype(BF16)
        for k in range(1, 16):
            remote(z_all.at[tile], z_all.at[tile], zg_s.at[k], zg_r.at[k], z_peer(k)[1]).start()

    for k in range(1, 16):
        @pl.when((z - k + 16) % 4 != 3)
        def _(k=k):
            remote(z_all.at[0], z_all.at[0], zg_s.at[k], zg_r.at[k], other).wait_recv()

    mine_at = HALF * core + PER * me
    total[pl.ds(mine_at, PER)] = z_all[...]
    gathers = []
    for k in range(1, 16):
        gathers.append(remote(z_all, total.at[pl.ds(mine_at, PER)], pg_s.at[k], pg_r.at[k], plane_peer(k)[1]))
    mirrors = [remote(z_all, total.at[pl.ds(mine_at, PER)], cg_s.at[0], cg_r.at[0], other)]
    for c in gathers + mirrors:
        c.start()

    for k in range(NJ):
        rims[3 + k].wait_recv()
    rim_near_copy.wait_recv()
    for c in sides:
        c.wait_recv()
    gm = gmixed[...].reshape(ROWS, PAD, D).astype(F32)
    for r in range(ROWS):
        gext[2 + r, WH:WH + PAD] += gm[r] + rim_far[r].astype(F32) + rim_near[r].astype(F32)
        east = side_in[0, r].astype(F32) + side_in[2, r].astype(F32) + side_in[4, r].astype(F32)
        east = pltpu.roll(jnp.concatenate([east, jnp.zeros((WH, D), F32)], axis=0), 4, 0)
        gext[2 + r, 176:208] += east
        gext[2 + r, 16:32] += side_in[1, r].astype(F32) + side_in[3, r].astype(F32) + side_in[5, r].astype(F32)
        gfield_ref[r] = gext[2 + r, WH:WH + LON].astype(BF16)

    for k in range(1, 16):
        gathers[k - 1].wait_recv()
        qx, qy = (x + 4 - k // 4) % 4, (y + 4 - k % 4) % 4
        at = pl.ds(HALF * core + PER * (qx * 4 + qy), PER)
        c = remote(total.at[at], total.at[at], cg_s.at[k], cg_r.at[k], other)
        c.start()
        mirrors.append(c)
    for c in mirrors:
        c.wait_recv()
    for n in range(3):
        gout_ref[:, 128 * n:128 * n + 128] = total[48 * n:48 * n + 48].reshape(HID, 128)
    for n in range(6):
        gin_ref[:, 128 * n:128 * n + 128] = total[144 + 24 * n:168 + 24 * n].reshape(D, 128)
    for b in range(K):
        folded = total[288 + 24 * b:312 + 24 * b].reshape(D, 128)
        gmix_ref[b] = folded[:, :DG].reshape(G, DG, DG)

    for c in sends[NJ:] + corners + rims + sides + [rim_near_copy, core_copy] + plane + gathers + mirrors:
        c.wait_send()
    for k in range(1, 16):
        @pl.when((z + k) % 4 != 3)
        def _(k=k):
            remote(z_out.at[0], z_in.at[k], z_s.at[k], z_r.at[k], other).wait_send()

        @pl.when(owner)
        def _(k=k):
            remote(z_all.at[0], z_all.at[0], zg_s.at[k], zg_r.at[k], other).wait_send()


def body(field, row_shift, output_tile_index, tiles, mix, w_in, w_out, cotangent):
    vmem = pl.BlockSpec(memory_space=pltpu.VMEM)
    smem = pl.BlockSpec(memory_space=pltpu.SMEM)
    dma = pltpu.SemaphoreType.DMA
    v = pltpu.VMEM
    return pl.pallas_call(
        kernel,
        name="block",
        out_shape=(
            jax.ShapeDtypeStruct((ROWS, LON, D), BF16),
            jax.ShapeDtypeStruct((ROWS, LON, D), BF16),
            jax.ShapeDtypeStruct((K, G, DG, DG), BF16),
            jax.ShapeDtypeStruct((D, HID), BF16),
            jax.ShapeDtypeStruct((HID, D), BF16),
        ),
        in_specs=[smem, smem] + [vmem] * 6,
        out_specs=[vmem] * 5,
        scratch_shapes=[
            v((6, EXT, D), BF16), v((6, WH, D), BF16), v((2, WH, D), BF16), v((2, PAD, D), BF16), v((ROWS, PAD, D), BF16),
            v((32, 128), F32), v((ROWS, K * JB, OFF * WIN), BF16), v((K * D, D), BF16), v((CELLS, K * D), BF16),
            v((CELLS, D), BF16), v((CELLS, HID), BF16), v((CELLS, HID), BF16), v((CELLS, HID), F32), v((CELLS, 256), F32),
            v((CELLS, D), BF16), v((CELLS, K * D), BF16), v((6, EXT, D), F32),
            v((6, PAD, D), BF16), v((2, PAD, D), BF16), v((2, PAD, D), BF16), v((2, PAD, D), BF16),
            v((2, 6, WH, D), BF16), v((6, 2, WH, D), BF16),
            v((TILES, 16, 128), BF16), v((HALF, 16, 128), BF16), v((HALF, 16, 128), BF16), v((16, PER, 16, 128), BF16),
            v((PER, 16, 128), F32), v((16, 16, 128), F32), v((PER, 16, 128), BF16), v((TILES, 16, 128), BF16),
            dma((13,)), dma((13,)), dma((13,)), dma((13,)), dma, dma,
            dma((16,)), dma((16,)), dma((16,)), dma((16,)), dma((16,)), dma((16,)), dma((16,)), dma((16,)), dma((16,)), dma((16,)),
        ],
        compiler_params=pltpu.CompilerParams(collective_id=0, has_side_effects=True, vmem_limit_bytes=48 * 2**20),
        cost_estimate=pl.CostEstimate(flops=4 * 10**9, bytes_accessed=8 * 10**6, transcendentals=3 * 10**5),
    )(row_shift, output_tile_index, field, cotangent, tiles, mix, w_in, w_out)


def solution(mesh):
    grid = P("lat", "lon", None)
    return jax.shard_map(
        body,
        mesh=mesh,
        in_specs=(grid, P("lat"), P("lat"), P(), P(), P(), P(), grid),
        out_specs=(grid, grid, P(), P(), P()),
        check_vma=False,
    )
```

time: 315 us -> 127 us (0.40)
  blocking collectives: 194 us -> 0 us
  Pallas kernels: 0 us -> 118 us
  starting transfers between devices: 57.7 us -> 0 us
  matrix products: 18.7 us -> 0 us
  local copies, waits for them, and re-layouts: 21.8 us -> 8.03 us
  waiting for transfers between devices: 13.5 us -> 0 us
  other arithmetic: 8.19 us -> 0 us
    psum x1 -> x0, blocking collectives: 194 us -> none  [body(): lax.psum((part_mix, input_portion, part_out), ('lat', 'lon'))]
    pallas_call x0 -> x1, Pallas kernels: none -> 118 us  [body(): pl.pallas_call(kernel, name='block', out_shape=(jax.ShapeDtypeStruct((ROW...]
    ppermute x8 -> x0, starting transfers between devices: 57.7 us -> none  [the longest x4 39.1 us: extended_2(): before = lax.ppermute(last, axis, up)]
    dot_general x12 -> x0, matrix products: 18.7 us -> none  [the longest x1 4.24 us: body(): jnp.einsum('tzsa,iwa->tzsiw', kernel_row_offsets, position_matrix, prefer...]
    ppermute x8 -> x0, waiting for transfers between devices: 13.5 us -> none  [the longest x4 8.26 us: extended_2(): before = lax.ppermute(last, axis, up)]
    slice x6 -> x0, local copies, waits for them, and re-layouts: 5.52 us -> none  [the longest x3 3.49 us: body(): rims = jnp.concatenate([core[:REACH], core[rows_here + REACH:]], axis=0)]
    scatter-add x2 -> x0, other arithmetic: 4.74 us -> none  [the longest x1 3.16 us: body(): jnp.zeros((rows_here + 2 * REACH, width, D), jnp.float32).at[row_index]]
    reshape x7 -> x0, local copies, waits for them, and re-layouts: 3.26 us -> none  [the longest x1 1.01 us: body(): output.reshape(rows_here, lon_here, D)]
  transfers between devices with their start and end apart: 8 -> 0, of which waited for: 3 -> 0; matrix products, arithmetic and copies ran while one was open for 5% -> 0% of each run, Pallas kernels for 0% -> 0%
where the time goes in v1:
time: 127 us
  Pallas kernels  118 us (93%)
  local copies, waits for them, and re-layouts  8.03 us (6%)
    pallas_call x1, Pallas kernels, body(): pl.pallas_call(kernel, name='block', out_shape=(jax.ShapeDtypeStruct((ROW...  118 us
    unnamed x16, local copies, waits for them, and re-layouts  6.19 us

profile of v1, /device:TPU:1, one launch (start us, length us, event | category | flops | bytes accessed | tf_op | source)
XLA Modules:
  0.0 127.0 jit_solution(3522716461071573622)
XLA Ops:
  0.6 0.0 copy-start.1
  0.6 0.0 copy-start
  0.7 0.9 copy.15.tiles_ref
  1.5 1.0 copy.13.field_ref
  2.5 0.0 copy-start.3
  2.5 0.0 copy-start.4
  2.6 1.0 copy.14.cot_ref
  3.6 0.0 copy-done.1
  3.6 0.0 copy-done
  3.6 0.0 copy-done.3
  3.6 0.0 copy-done.4
  3.6 0.0 copy-start.2
  3.6 1.0 copy-done.2
  4.6 118.2 %block.1 = (bf16[2,180,384]{2,1,0:T(8,128)(2,1)S(1)}, bf16[2,180,384]{2,1,0:T(8,128)(2,1)S(1)}, bf16[3,4,96,96]{3,2,1,0:T(8,128)(2,1)S(1)}, bf16[384,768]{1,0:T(8,128)(2,1)S(1)}, bf16[768,384]{1,0:T(8,128)(2,1)S(1)}) custom-call(s32[2]{0:T(128)S(1)} %copy-done.3, s32[2]{0:T(128)S(1)} %copy-done.4, bf16[2,180,384]{2,1,0:T(8,128)(2,1)S(1)} %copy.13.field_ref, ...), custom_call_target="tpu_custom_call" | custom-call | flops 4000000000 | bytes 8000000 | tf_op jit(solution)/shard_map/block/pallas_call | solution.py:369
  122.8 0.9 copy.16
  123.7 0.9 copy.17
  124.6 0.7 copy.21
  125.3 0.8 copy.22
  126.2 0.8 copy.23
Async XLA Ops:
  0.6 2.9 %copy-start.1 = (bf16[768,384]{1,0:T(8,128)(2,1)S(1)}, bf16[768,384]{1,0:T(8,128)(2,1)}, u32[]{:S(2)}) copy-start(bf16[768,384]{1,0:T(8,128)(2,1)} %wout_ref.1) | copy-start | bytes 1769476
  0.6 2.9 %copy-start = (bf16[384,768]{1,0:T(8,128)(2,1)S(1)}, bf16[384,768]{1,0:T(8,128)(2,1)}, u32[]{:S(2)}) copy-start(bf16[384,768]{1,0:T(8,128)(2,1)} %win_ref.1) | copy-start | bytes 1769476
  2.5 1.0 copy-start.3
  2.5 1.0 copy-start.4
  3.6 1.0 copy-start.2

commit v2 on v1

v2 whole, which is shorter than its diff:
```python
import functools

import jax
import jax.numpy as jnp
from jax import lax
from jax.experimental import pallas as pl
from jax.experimental.pallas import tpu as pltpu
from jax.sharding import PartitionSpec as P

D = 384
HID = 768
G = 4
DG = 96
K = 3
WTAP = 33
NLAT = 128
WH = 16
ROWS = 2
LON = 180
PAD = 192
JB = 64
NJ = 3
MID = 48
EARLY = 2
WIN = 128
EXT = 256
OFF = 5
CELLS = ROWS * PAD
TILES = 384
PIECE = TILES // 2
HALF = PIECE // 2
PER = HALF // 16
MESH = pl.DeviceIdType.MESH
F32 = jnp.float32
BF16 = jnp.bfloat16


def dot(a, b, contract=((1,), (0,))):
    return lax.dot_general(a, b, (contract, ((), ())), preferred_element_type=F32)


def position():
    lat, lon = lax.axis_index("lat"), lax.axis_index("lon")
    return lat // 16, (lat // 4) % 4, ((lat // 2) % 2) * 8 + lon, lat % 2


def device(x, y, z, core):
    return (((x * 4 + y) * 2 + z // 8) * 2 + core, z % 8)


def remote(src, dst, send_sem, recv_sem, to):
    return pltpu.make_async_remote_copy(
        src_ref=src, dst_ref=dst, send_sem=send_sem, recv_sem=recv_sem, device_id=to, device_id_type=MESH
    )


class Halo:
    def __init__(self, sems_out, sems_in):
        lat, lon = lax.axis_index("lat"), lax.axis_index("lon")
        core = lat % 2
        step = 1 - 2 * core
        self.near = (lat + step, lon)
        self.far = ((lat + 64 - step) % 64, lon)
        west, east = (lon + 7) % 8, (lon + 1) % 8
        self.west, self.east = (lat, west), (lat, east)
        self.near_west, self.near_east = (lat + step, west), (lat + step, east)
        self.sems_out, self.sems_in = sems_out, sems_in

    def copy(self, i, src, dst, to):
        return remote(src, dst, self.sems_out.at[i], self.sems_in.at[i], to)


def kernel(
    shift_ref, index_ref, field_ref, cot_ref, tiles_ref, mix_ref, win_ref, wout_ref,
    out_ref, gfield_ref, gmix_ref, gin_ref, gout_ref,
    ext, east_in, east_out, far_east, tail_out, tail_in, cot, taps, strip, mixd, basis, mixed, hidden, gpre, ghid, pre,
    gmixed, gbasis, gext, rim_mid, far_mid, rim_ends, far_ends, rim_tail, far_tail, rim_near_out, rim_near, side_out, side_in,
    part, core_in, half_out, plane_in, z_out, z_in, z_all, total,
    halo_s, halo_r, rim_s, rim_r, core_s, core_r, plane_s, plane_r, z_s, z_r, zg_s, zg_r, pg_s, pg_r, cg_s, cg_r,
):
    x, y, z, core = position()
    lat, lon = lax.axis_index("lat"), lax.axis_index("lon")
    halo = Halo(halo_s, halo_r)
    other = device(x, y, z, 1 - core)

    def plane_peer(k):
        px, py = (x + k // 4) % 4, (y + k % 4) % 4
        return px * 4 + py, device(px, py, z, core)

    def z_peer(k):
        pz = (z + k) % 16
        return pz, device(x, y, pz, core)

    barrier = pltpu.get_barrier_semaphore()
    greet = [halo.near, halo.far, halo.west, halo.east, halo.near_west, halo.near_east]
    greet += [plane_peer(k)[1] for k in range(1, 16)] + [z_peer(k)[1] for k in range(1, 16)]
    for to in greet:
        pl.semaphore_signal(barrier, inc=1, device_id=to, device_id_type=MESH)

    ext[2:4, PAD:EXT] = jnp.zeros((2, EXT - PAD, D), BF16)
    for r in (0, 1, 4, 5):
        ext[r, WH + PAD:EXT] = jnp.zeros((EXT - WH - PAD, D), BF16)
    for r in range(ROWS):
        ext[2 + r, WH:WH + LON] = field_ref[r]
        cot[r, PAD - 16:PAD] = jnp.zeros((16, D), BF16)
        cot[r, 0:LON] = cot_ref[r]
        edge = ext[2 + r, 176:208].astype(F32)
        east_out[r] = pltpu.roll(edge, 28, 0)[:WH].astype(BF16)
    tails = [ext[2 + r, 192:208].astype(F32) for r in range(ROWS)]
    tail_out[...] = (tails[0] + pltpu.roll(tails[1], 4, 0)).astype(BF16)

    ghid[...] = dot(cot[...].reshape(CELLS, D), wout_ref[...], ((1,), (1,)))
    group = lambda n: (n >= DG).astype(jnp.int32) + (n >= 2 * DG).astype(jnp.int32) + (n >= 3 * DG).astype(jnp.int32)
    row_i, col_i = (lax.broadcasted_iota(jnp.int32, (D, D), d) for d in (0, 1))
    block = group(row_i) == group(col_i)
    s_row, s_col = (lax.broadcasted_iota(jnp.int32, (DG, D), d) for d in (0, 1))
    spread = (s_row == s_col - DG * group(s_col)).astype(BF16)
    for b in range(K):
        wide = dot(mix_ref[b].reshape(D, DG), spread)
        mixd[D * b:D * b + D] = jnp.where(block, wide, 0.0).astype(BF16)
    taps[...] = jnp.zeros((32, 128), F32)
    for r in range(ROWS):
        s, t = shift_ref[r], index_ref[r]
        for b in range(K):
            tile = tiles_ref[b, t].astype(F32)
            for o in range(OFF):
                line = jnp.zeros((1, WTAP), F32)
                here = lat * ROWS + r + o - 2
                inside = jnp.logical_and(here >= 0, here < NLAT)
                for k in range(K):
                    line = jnp.where(jnp.logical_and(inside, k == o - 1 - s), tile[k:k + 1], line)
                n = (r * K + b) * OFF + o
                taps[n:n + 1, 0:WTAP] = line
    for r in range(ROWS):
        for b in range(K):
            for o in range(OFF):
                n = (r * K + b) * OFF + o
                line = jnp.broadcast_to(taps[n:n + 1], (JB, WIN))
                strip[r, JB * b:JB * b + JB, WIN * o:WIN * o + WIN] = pltpu.roll(
                    line, 0, 1, stride=1, stride_axis=0).astype(BF16)

    pl.semaphore_wait(barrier, len(greet))

    near_at = core * 4
    far_at = 4 - core * 4
    far_here = pl.ds(core * 4, 2)
    send_w = halo.copy(3, ext.at[2:4, 16:32], ext.at[pl.ds(far_at, 2), 16:32], halo.far)
    send_e = halo.copy(4, ext.at[2:4, 176:192], ext.at[pl.ds(far_at, 2), 176:192], halo.far)
    send_t = halo.copy(5, tail_out, tail_in, halo.far)
    sends = [send_e, send_t, send_w]
    for k in range(NJ):
        at = pl.ds(2 * WH + MID * k, MID)
        sends.append(halo.copy(k, ext.at[2:4, at], ext.at[pl.ds(far_at, 2), at], halo.far))
    near = halo.copy(6, ext.at[2:4, WH:WH + PAD], ext.at[pl.ds(near_at, 2), WH:WH + PAD], halo.near)
    own_west = ext.at[2:4, 16:32]
    corners = [
        halo.copy(9, own_west, east_in.at[2:4], halo.west),
        halo.copy(10, east_out, ext.at[2:4, 0:16], halo.east),
        halo.copy(11, own_west, east_in.at[pl.ds(near_at, 2)], halo.near_west),
        halo.copy(12, east_out, ext.at[pl.ds(near_at, 2), 0:16], halo.near_east),
    ]
    for c in sends + [near] + corners:
        c.start()

    send_w.wait_recv()
    pass_w = halo.copy(7, ext.at[far_here, 16:32], east_in.at[far_here], halo.west)
    pass_w.start()
    send_e.wait_recv()
    send_t.wait_recv()
    four = lax.broadcasted_iota(jnp.int32, (WH, D), 0) < 4
    tail = tail_in[...].astype(F32)
    for r in range(ROWS):
        end = jnp.where(four, tail if r == 0 else pltpu.roll(tail, 12, 0), 0.0)
        ext[core * 4 + r, 192:208] = end.astype(BF16)
        edge = jnp.concatenate([ext[core * 4 + r, 176:192].astype(F32), end], axis=0)
        far_east[r] = pltpu.roll(edge, 28, 0)[:WH].astype(BF16)
    pass_e = halo.copy(8, far_east, ext.at[far_here, 0:16], halo.east)
    pass_e.start()

    near.wait()
    for c in sends[3:] + corners + [pass_w, pass_e]:
        c.wait_recv()
    for r in range(6):
        edge = jnp.concatenate([east_in[r].astype(F32), jnp.zeros((WH, D), F32)], axis=0)
        ext[r, PAD:PAD + 32] = (ext[r, PAD:PAD + 32].astype(F32) + pltpu.roll(edge, 4, 0)).astype(BF16)

    for r in range(ROWS):
        for j in range(NJ):
            window = ext[r:r + OFF, JB * j:JB * j + WIN].reshape(OFF * WIN, D)
            found = dot(strip[r], window).astype(BF16)
            for b in range(K):
                basis[r * PAD + JB * j:r * PAD + JB * j + JB, D * b:D * b + D] = found[JB * b:JB * b + JB]
    own = ext[2:4, WH:WH + PAD].reshape(CELLS, D).astype(F32)
    mixed[...] = (own + dot(basis[...], mixd[...])).astype(BF16)

    c0, c1 = 0.7978845608028654, 0.044715
    for n in range(3):
        pre[...] = dot(mixed[...], win_ref[:, 256 * n:256 * n + 256])

        def step(i, carry, n=n):
            at = pl.ds(pl.multiple_of(i * 64, 64), 64)
            p = pre[at, :]
            sq = p * p
            t = jnp.tanh(c0 * p * (1.0 + c1 * sq))
            half = 0.5 * (1.0 + t)
            hidden[at, 256 * n:256 * n + 256] = (p * half).astype(BF16)
            slope = half + 0.5 * p * (1.0 - t * t) * (c0 * (1.0 + 3.0 * c1 * sq))
            gpre[at, 256 * n:256 * n + 256] = (ghid[at, 256 * n:256 * n + 256] * slope).astype(BF16)
            return carry

        lax.fori_loop(0, CELLS // 64, step, 0)

    gmixed[...] = (cot[...].reshape(CELLS, D).astype(F32) + dot(gpre[...], win_ref[...], ((1,), (1,)))).astype(BF16)
    for b in range(K):
        gbasis[:, D * b:D * b + D] = dot(gmixed[...], mixd[D * b:D * b + D], ((1,), (1,))).astype(BF16)
    gext[...] = jnp.zeros((6, EXT, D), F32)
    for r in range(ROWS):
        for j in range(NJ):
            at = r * PAD + JB * j
            lines = jnp.concatenate([gbasis[at:at + JB, D * b:D * b + D] for b in range(K)], axis=0)
            piece = dot(strip[r], lines, ((0,), (0,)))
            gext[r:r + OFF, JB * j:JB * j + WIN] += piece.reshape(OFF, WIN, D)
    for r in range(6):
        side_out[0, r] = gext[r, 0:WH].astype(BF16)
        side_out[1, r] = pltpu.roll(gext[r, PAD:PAD + 32], 28, 0)[:WH].astype(BF16)
    for r in range(ROWS):
        rim_mid[r] = gext[core * 4 + r, 2 * WH:2 * WH + NJ * MID].astype(BF16)
    rim = Halo(rim_s, rim_r)
    rims = [rim.copy(9, side_out.at[0], side_in.at[0], rim.west), rim.copy(10, side_out.at[1], side_in.at[1], rim.east)]
    for k in range(NJ):
        at = pl.ds(MID * k, MID)
        rims.append(rim.copy(k, rim_mid.at[:, at], far_mid.at[:, at], rim.far))
    for c in rims[:2 + EARLY]:
        c.start()

    def core_send(p):
        c = remote(part.at[pl.ds(PIECE * p + HALF * (1 - core), HALF)], core_in.at[p], core_s.at[p], core_r.at[p], other)
        c.start()
        return c

    cots = cot[...].reshape(CELLS, D)
    d_out = dot(hidden[...], cots, ((0,), (0,))).astype(BF16)
    for n in range(3):
        part[48 * n:48 * n + 48] = d_out[:, 128 * n:128 * n + 128].reshape(48, 16, 128)

    def pack_in(n):
        d_in = dot(mixed[...], gpre[:, 256 * n:256 * n + 256], ((0,), (0,))).astype(BF16)
        for h in range(2):
            at = 144 + 24 * (2 * n + h)
            part[at:at + 24] = d_in[:, 128 * h:128 * h + 128].reshape(24, 16, 128)

    pack_in(0)
    core_copies = [core_send(0)]
    pack_in(1)
    pack_in(2)
    f_row, f_col = (lax.broadcasted_iota(jnp.int32, (D, 128), d) for d in (0, 1))
    fold = (f_col == f_row - DG * group(f_row)).astype(BF16)
    for b in range(K):
        d_mix = dot(basis[:, D * b:D * b + D], gmixed[...], ((0,), (0,)))
        d_mix = jnp.where(block, d_mix, 0.0).astype(BF16)
        part[288 + 24 * b:312 + 24 * b] = dot(d_mix, fold).astype(BF16).reshape(24, 16, 128)
    part[360:TILES] = jnp.zeros((TILES - 360, 16, 128), BF16)
    core_copies.append(core_send(1))

    me = x * 4 + y

    def core_sum(p, q):
        mine = part[pl.ds(PIECE * p + HALF * core + PER * q, PER)].astype(F32)
        return mine + core_in[p, pl.ds(PER * q, PER)].astype(F32)

    def plane_send(p):
        core_copies[p].wait_recv()
        copies = []
        for k in range(1, 16):
            q, to = plane_peer(k)
            half_out[p, pl.ds(PER * q, PER)] = core_sum(p, q).astype(BF16)
            c = remote(half_out.at[p, pl.ds(PER * q, PER)], plane_in.at[p, k], plane_s.at[p, k], plane_r.at[p, k], to)
            c.start()
            copies.append(c)
        z_out[p] = core_sum(p, me)
        return copies

    plane = [plane_send(0)]

    plane.append(plane_send(1))

    out = mixed[...].astype(F32) + dot(hidden[...], wout_ref[...])
    for r in range(ROWS):
        out_ref[r] = out[r * PAD:r * PAD + LON].astype(BF16)

    for c in rims[:2]:
        c.wait_recv()
    for r in range(6):
        gext[r, WH:2 * WH] += side_in[1, r].astype(F32)
        edge = jnp.concatenate([side_in[0, r].astype(F32), jnp.zeros((WH, D), F32)], axis=0)
        gext[r, 176:208] += pltpu.roll(edge, 4, 0)
    ends = []
    for r in range(ROWS):
        rim_near_out[r] = gext[4 - core * 4 + r, WH:WH + PAD].astype(BF16)
        rim_ends[0, r] = gext[core * 4 + r, WH:2 * WH].astype(BF16)
        rim_ends[1, r] = gext[core * 4 + r, 176:192].astype(BF16)
        ends.append(jnp.where(four, gext[core * 4 + r, 192:208], 0.0))
    rim_tail[...] = (ends[0] + pltpu.roll(ends[1], 4, 0)).astype(BF16)
    rims += [
        rim.copy(3, rim_ends, far_ends, rim.far),
        rim.copy(5, rim_tail, far_tail, rim.far),
        rim.copy(6, rim_near_out, rim_near, rim.near),
    ]
    rims[-1].start()

    def owns(p, at):
        return (at % 8 + 3 - p) % 3 == 0

    def tile_of(p, at):
        return jnp.minimum((at // 8) * 3 + jnp.maximum(at % 8 - p, 0) // 3, PER - 1)

    def z_send(p):
        for c in plane[p]:
            c.wait_recv()
        acc = z_out[p]
        for k in range(1, 16):
            acc += plane_in[p, k].astype(F32)
        z_out[p] = acc
        for k in range(1, 16):
            pz, to = z_peer(k)

            @pl.when(owns(p, pz))
            def _(k=k, pz=pz, to=to):
                remote(z_out.at[p, tile_of(p, pz)], z_in.at[p, k], z_s.at[p, k], z_r.at[p, k], to).start()

    def z_sum(p):
        tile = tile_of(p, z)

        @pl.when(owns(p, z))
        def _():
            for k in range(1, 16):
                remote(z_out.at[p, 0], z_in.at[p, k], z_s.at[p, k], z_r.at[p, k], other).wait_recv()
            acc = z_out[p, tile]
            for k in range(1, 16):
                acc += z_in[p, k]
            z_all[p, tile] = acc.astype(BF16)
            for k in range(1, 16):
                remote(z_all.at[p, tile], z_all.at[p, tile], zg_s.at[p, k], zg_r.at[p, k], z_peer(k)[1]).start()

    def mine_at(p):
        return pl.ds(PIECE * p + HALF * core + PER * me, PER)

    def gather_send(p):
        for k in range(1, 16):
            @pl.when(owns(p, (z - k + 16) % 16))
            def _(k=k):
                remote(z_all.at[p, 0], z_all.at[p, 0], zg_s.at[p, k], zg_r.at[p, k], other).wait_recv()

        total[mine_at(p)] = z_all[p]
        copies = []
        for k in range(1, 16):
            to = plane_peer(k)[1]
            copies.append(remote(z_all.at[p], total.at[mine_at(p)], pg_s.at[p, k], pg_r.at[p, k], to))
        copies.append(remote(z_all.at[p], total.at[mine_at(p)], cg_s.at[p, 0], cg_r.at[p, 0], other))
        for c in copies:
            c.start()
        return copies[:15], copies[15:]

    z_send(0)
    z_send(1)
    z_sum(0)
    z_sum(1)
    for c in rims[2 + EARLY:-1]:
        c.start()
    gathers = [gather_send(0)]
    gathers.append(gather_send(1))

    for c in rims[2:]:
        c.wait_recv()
    gm = gmixed[...].reshape(ROWS, PAD, D).astype(F32)
    tail = far_tail[...].astype(F32)
    for r in range(ROWS):
        gext[2 + r, WH:WH + PAD] += gm[r] + rim_near[r].astype(F32)
        gext[2 + r, WH:2 * WH] += far_ends[0, r].astype(F32)
        gext[2 + r, 2 * WH:176] += far_mid[r].astype(F32)
        gext[2 + r, 176:192] += far_ends[1, r].astype(F32)
        gext[2 + r, 192:208] += tail if r == 0 else pltpu.roll(tail, 12, 0)
        gfield_ref[r] = gext[2 + r, WH:WH + LON].astype(BF16)

    mirrors = gathers[0][1] + gathers[1][1]
    for p in range(2):
        for k in range(1, 16):
            gathers[p][0][k - 1].wait_recv()
            qx, qy = (x + 4 - k // 4) % 4, (y + 4 - k % 4) % 4
            at = pl.ds(PIECE * p + HALF * core + PER * (qx * 4 + qy), PER)
            c = remote(total.at[at], total.at[at], cg_s.at[p, k], cg_r.at[p, k], other)
            c.start()
            mirrors.append(c)
    for c in mirrors:
        c.wait_recv()
    for n in range(3):
        gout_ref[:, 128 * n:128 * n + 128] = total[48 * n:48 * n + 48].reshape(HID, 128)
    for n in range(6):
        gin_ref[:, 128 * n:128 * n + 128] = total[144 + 24 * n:168 + 24 * n].reshape(D, 128)
    for b in range(K):
        folded = total[288 + 24 * b:312 + 24 * b].reshape(D, 128)
        gmix_ref[b] = folded[:, :DG].reshape(G, DG, DG)

    for c in sends + corners + [pass_w, pass_e] + rims + core_copies + plane[0] + plane[1] + gathers[0][0] + gathers[1][0] + mirrors:
        c.wait_send()
    for p in range(2):
        for k in range(1, 16):
            @pl.when(owns(p, (z + k) % 16))
            def _(p=p, k=k):
                remote(z_out.at[p, 0], z_in.at[p, k], z_s.at[p, k], z_r.at[p, k], other).wait_send()

            @pl.when(owns(p, z))
            def _(p=p, k=k):
                remote(z_all.at[p, 0], z_all.at[p, 0], zg_s.at[p, k], zg_r.at[p, k], other).wait_send()


def body(field, row_shift, output_tile_index, tiles, mix, w_in, w_out, cotangent):
    vmem = pl.BlockSpec(memory_space=pltpu.VMEM)
    smem = pl.BlockSpec(memory_space=pltpu.SMEM)
    dma = pltpu.SemaphoreType.DMA
    v = pltpu.VMEM
    return pl.pallas_call(
        kernel,
        name="block",
        out_shape=(
            jax.ShapeDtypeStruct((ROWS, LON, D), BF16),
            jax.ShapeDtypeStruct((ROWS, LON, D), BF16),
            jax.ShapeDtypeStruct((K, G, DG, DG), BF16),
            jax.ShapeDtypeStruct((D, HID), BF16),
            jax.ShapeDtypeStruct((HID, D), BF16),
        ),
        in_specs=[smem, smem] + [vmem] * 6,
        out_specs=[vmem] * 5,
        scratch_shapes=[
            v((6, EXT, D), BF16), v((6, WH, D), BF16), v((2, WH, D), BF16), v((2, WH, D), BF16), v((WH, D), BF16), v((WH, D), BF16),
            v((ROWS, PAD, D), BF16),
            v((32, 128), F32), v((ROWS, K * JB, OFF * WIN), BF16), v((K * D, D), BF16), v((CELLS, K * D), BF16),
            v((CELLS, D), BF16), v((CELLS, HID), BF16), v((CELLS, HID), BF16), v((CELLS, HID), F32), v((CELLS, 256), F32),
            v((CELLS, D), BF16), v((CELLS, K * D), BF16), v((6, EXT, D), F32),
            v((2, NJ * MID, D), BF16), v((2, NJ * MID, D), BF16), v((2, 2, WH, D), BF16), v((2, 2, WH, D), BF16),
            v((WH, D), BF16), v((WH, D), BF16), v((2, PAD, D), BF16), v((2, PAD, D), BF16),
            v((2, 6, WH, D), BF16), v((2, 6, WH, D), BF16),
            v((TILES, 16, 128), BF16), v((2, HALF, 16, 128), BF16), v((2, HALF, 16, 128), BF16),
            v((2, 16, PER, 16, 128), BF16), v((2, PER, 16, 128), F32), v((2, 16, 16, 128), F32),
            v((2, PER, 16, 128), BF16), v((TILES, 16, 128), BF16),
            dma((13,)), dma((13,)), dma((13,)), dma((13,)), dma((2,)), dma((2,)),
        ] + [dma((2, 16))] * 10,
        compiler_params=pltpu.CompilerParams(collective_id=0, has_side_effects=True, vmem_limit_bytes=48 * 2**20),
        cost_estimate=pl.CostEstimate(flops=4 * 10**9, bytes_accessed=8 * 10**6, transcendentals=3 * 10**5),
    )(row_shift, output_tile_index, field, cotangent, tiles, mix, w_in, w_out)


def solution(mesh):
    grid = P("lat", "lon", None)
    return jax.shard_map(
        body,
        mesh=mesh,
        in_specs=(grid, P("lat"), P("lat"), P(), P(), P(), P(), grid),
        out_specs=(grid, grid, P(), P(), P()),
        check_vma=False,
    )
```

time: 127 us -> 123 us (0.969)
  Pallas kernels: 118 us -> 114 us
    pallas_call x1, Pallas kernels: 118 us -> 114 us  [body(): pl.pallas_call(kernel, name='block', out_shape=(jax.ShapeDtypeStruct((ROW...]
where the time goes in v2:
time: 123 us
  Pallas kernels  114 us (93%)
  local copies, waits for them, and re-layouts  8.03 us (7%)
    pallas_call x1, Pallas kernels, body(): pl.pallas_call(kernel, name='block', out_shape=(jax.ShapeDtypeStruct((ROW...  114 us
    unnamed x16, local copies, waits for them, and re-layouts  6.19 us

profile of v2, /device:TPU:1, one launch (start us, length us, event | category | flops | bytes accessed | tf_op | source)
XLA Modules:
  0.0 122.6 jit_solution(11921704365138901193)
XLA Ops:
  0.6 0.0 copy-start.1
  0.6 0.0 copy-start
  0.7 0.9 copy.15.tiles_ref
  1.5 1.0 copy.13.field_ref
  2.5 0.0 copy-start.3
  2.5 0.0 copy-start.4
  2.6 1.0 copy.14.cot_ref
  3.6 0.0 copy-done.1
  3.6 0.0 copy-done
  3.6 0.0 copy-done.3
  3.6 0.0 copy-done.4
  3.6 0.0 copy-start.2
  3.6 1.0 copy-done.2
  4.6 113.8 %block.1 = (bf16[2,180,384]{2,1,0:T(8,128)(2,1)S(1)}, bf16[2,180,384]{2,1,0:T(8,128)(2,1)S(1)}, bf16[3,4,96,96]{3,2,1,0:T(8,128)(2,1)S(1)}, bf16[384,768]{1,0:T(8,128)(2,1)S(1)}, bf16[768,384]{1,0:T(8,128)(2,1)S(1)}) custom-call(s32[2]{0:T(128)S(1)} %copy-done.3, s32[2]{0:T(128)S(1)} %copy-done.4, bf16[2,180,384]{2,1,0:T(8,128)(2,1)S(1)} %copy.13.field_ref, ...), custom_call_target="tpu_custom_call" | custom-call | flops 4000000000 | bytes 8000000 | tf_op jit(solution)/shard_map/block/pallas_call | solution.py:422
  118.4 0.9 copy.16
  119.3 0.9 copy.17
  120.2 0.7 copy.21
  120.9 0.8 copy.22
  121.8 0.8 copy.23
Async XLA Ops:
  0.6 2.9 %copy-start.1 = (bf16[768,384]{1,0:T(8,128)(2,1)S(1)}, bf16[768,384]{1,0:T(8,128)(2,1)}, u32[]{:S(2)}) copy-start(bf16[768,384]{1,0:T(8,128)(2,1)} %wout_ref.1) | copy-start | bytes 1769476
  0.6 2.9 %copy-start = (bf16[384,768]{1,0:T(8,128)(2,1)S(1)}, bf16[384,768]{1,0:T(8,128)(2,1)}, u32[]{:S(2)}) copy-start(bf16[384,768]{1,0:T(8,128)(2,1)} %win_ref.1) | copy-start | bytes 1769476
  2.5 1.0 copy-start.3
  2.5 1.0 copy-start.4
  3.6 1.0 copy-start.2

commit v3 on v2

--- a/solution.py
+++ b/solution.py
@@ -63,7 +63,6 @@
         self.far = ((lat + 64 - step) % 64, lon)
         west, east = (lon + 7) % 8, (lon + 1) % 8
         self.west, self.east = (lat, west), (lat, east)
-        self.near_west, self.near_east = (lat + step, west), (lat + step, east)
         self.sems_out, self.sems_in = sems_out, sems_in
 
     def copy(self, i, src, dst, to):
@@ -71,11 +70,12 @@
 
 
 def kernel(
-    shift_ref, index_ref, field_ref, cot_ref, tiles_ref, mix_ref, win_ref, wout_ref,
-    out_ref, gfield_ref, gmix_ref, gin_ref, gout_ref,
+    shift_ref, index_ref, field_hbm, cot_hbm, tiles_ref, mix_hbm, win_hbm, wout_hbm,
+    out_ref, gfield_ref, total,
+    field_ref, cot_ref, mix_ref, win_ref, wout_ref, load_s,
     ext, east_in, east_out, far_east, tail_out, tail_in, cot, taps, strip, mixd, basis, mixed, hidden, gpre, ghid, pre,
     gmixed, gbasis, gext, rim_mid, far_mid, rim_ends, far_ends, rim_tail, far_tail, rim_near_out, rim_near, side_out, side_in,
-    part, core_in, half_out, plane_in, z_out, z_in, z_all, total,
+    part, core_in, half_out, plane_in, z_out, z_in, z_all,
     halo_s, halo_r, rim_s, rim_r, core_s, core_r, plane_s, plane_r, z_s, z_r, zg_s, zg_r, pg_s, pg_r, cg_s, cg_r,
 ):
     x, y, z, core = position()
@@ -92,29 +92,41 @@
         return pz, device(x, y, pz, core)
 
     barrier = pltpu.get_barrier_semaphore()
-    greet = [halo.near, halo.far, halo.west, halo.east, halo.near_west, halo.near_east]
+    greet = [halo.near, halo.far, halo.west, halo.east]
     greet += [plane_peer(k)[1] for k in range(1, 16)] + [z_peer(k)[1] for k in range(1, 16)]
     for to in greet:
         pl.semaphore_signal(barrier, inc=1, device_id=to, device_id_type=MESH)
 
+    loads = [
+        pltpu.make_async_copy(src, dst, load_s.at[i])
+        for i, (src, dst) in enumerate([
+            (field_hbm, field_ref), (cot_hbm, cot_ref), (wout_hbm, wout_ref), (mix_hbm, mix_ref), (win_hbm, win_ref)])
+    ]
+    for c in loads:
+        c.start()
     ext[2:4, PAD:EXT] = jnp.zeros((2, EXT - PAD, D), BF16)
     for r in (0, 1, 4, 5):
         ext[r, WH + PAD:EXT] = jnp.zeros((EXT - WH - PAD, D), BF16)
     for r in range(ROWS):
-        ext[2 + r, WH:WH + LON] = field_ref[r]
         cot[r, PAD - 16:PAD] = jnp.zeros((16, D), BF16)
-        cot[r, 0:LON] = cot_ref[r]
+    loads[0].wait()
+    ext[2:4, WH:WH + LON] = jnp.swapaxes(field_ref[...], 0, 1)
+    for r in range(ROWS):
         edge = ext[2 + r, 176:208].astype(F32)
         east_out[r] = pltpu.roll(edge, 28, 0)[:WH].astype(BF16)
     tails = [ext[2 + r, 192:208].astype(F32) for r in range(ROWS)]
     tail_out[...] = (tails[0] + pltpu.roll(tails[1], 4, 0)).astype(BF16)
 
+    loads[1].wait()
+    cot[:, 0:LON] = jnp.swapaxes(cot_ref[...], 0, 1)
+    loads[2].wait()
     ghid[...] = dot(cot[...].reshape(CELLS, D), wout_ref[...], ((1,), (1,)))
     group = lambda n: (n >= DG).astype(jnp.int32) + (n >= 2 * DG).astype(jnp.int32) + (n >= 3 * DG).astype(jnp.int32)
     row_i, col_i = (lax.broadcasted_iota(jnp.int32, (D, D), d) for d in (0, 1))
     block = group(row_i) == group(col_i)
     s_row, s_col = (lax.broadcasted_iota(jnp.int32, (DG, D), d) for d in (0, 1))
     spread = (s_row == s_col - DG * group(s_col)).astype(BF16)
+    loads[3].wait()
     for b in range(K):
         wide = dot(mix_ref[b].reshape(D, DG), spread)
         mixd[D * b:D * b + D] = jnp.where(block, wide, 0.0).astype(BF16)
@@ -122,13 +134,15 @@
     for r in range(ROWS):
         s, t = shift_ref[r], index_ref[r]
         for b in range(K):
-            tile = tiles_ref[b, t].astype(F32)
+            chosen = lax.broadcasted_iota(jnp.int32, (16, WTAP), 0) == t
+            tile = [
+                jnp.sum(jnp.where(chosen, tiles_ref[b, k].astype(F32), 0.0), axis=0, keepdims=True) for k in range(K)]
             for o in range(OFF):
                 line = jnp.zeros((1, WTAP), F32)
                 here = lat * ROWS + r + o - 2
                 inside = jnp.logical_and(here >= 0, here < NLAT)
                 for k in range(K):
-                    line = jnp.where(jnp.logical_and(inside, k == o - 1 - s), tile[k:k + 1], line)
+                    line = jnp.where(jnp.logical_and(inside, k == o - 1 - s), tile[k], line)
                 n = (r * K + b) * OFF + o
                 taps[n:n + 1, 0:WTAP] = line
     for r in range(ROWS):
@@ -139,6 +153,8 @@
                 strip[r, JB * b:JB * b + JB, WIN * o:WIN * o + WIN] = pltpu.roll(
                     line, 0, 1, stride=1, stride_axis=0).astype(BF16)
 
+    gext[...] = jnp.zeros((6, EXT, D), F32)
+    loads[4].wait()
     pl.semaphore_wait(barrier, len(greet))
 
     near_at = core * 4
@@ -156,12 +172,16 @@
     corners = [
         halo.copy(9, own_west, east_in.at[2:4], halo.west),
         halo.copy(10, east_out, ext.at[2:4, 0:16], halo.east),
-        halo.copy(11, own_west, east_in.at[pl.ds(near_at, 2)], halo.near_west),
-        halo.copy(12, east_out, ext.at[pl.ds(near_at, 2), 0:16], halo.near_east),
     ]
     for c in sends + [near] + corners:
         c.start()
 
+    corners[0].wait_recv()
+    share_w = halo.copy(11, east_in.at[2:4], east_in.at[pl.ds(near_at, 2)], halo.near)
+    share_w.start()
+    corners[1].wait_recv()
+    share_e = halo.copy(12, ext.at[2:4, 0:16], ext.at[pl.ds(near_at, 2), 0:16], halo.near)
+    share_e.start()
     send_w.wait_recv()
     pass_w = halo.copy(7, ext.at[far_here, 16:32], east_in.at[far_here], halo.west)
     pass_w.start()
@@ -178,7 +198,7 @@
     pass_e.start()
 
     near.wait()
-    for c in sends[3:] + corners + [pass_w, pass_e]:
+    for c in sends[3:] + [share_w, share_e, pass_w, pass_e]:
         c.wait_recv()
     for r in range(6):
         edge = jnp.concatenate([east_in[r].astype(F32), jnp.zeros((WH, D), F32)], axis=0)
@@ -213,16 +233,24 @@
     gmixed[...] = (cot[...].reshape(CELLS, D).astype(F32) + dot(gpre[...], win_ref[...], ((1,), (1,)))).astype(BF16)
     for b in range(K):
         gbasis[:, D * b:D * b + D] = dot(gmixed[...], mixd[D * b:D * b + D], ((1,), (1,))).astype(BF16)
-    gext[...] = jnp.zeros((6, EXT, D), F32)
-    for r in range(ROWS):
+
+    def adjoint(r, first, last):
         for j in range(NJ):
             at = r * PAD + JB * j
             lines = jnp.concatenate([gbasis[at:at + JB, D * b:D * b + D] for b in range(K)], axis=0)
-            piece = dot(strip[r], lines, ((0,), (0,)))
-            gext[r:r + OFF, JB * j:JB * j + WIN] += piece.reshape(OFF, WIN, D)
-    for r in range(6):
-        side_out[0, r] = gext[r, 0:WH].astype(BF16)
-        side_out[1, r] = pltpu.roll(gext[r, PAD:PAD + 32], 28, 0)[:WH].astype(BF16)
+            piece = dot(strip[r, :, WIN * first:WIN * last], lines, ((0,), (0,)))
+            gext[r + first:r + last, JB * j:JB * j + WIN] += piece.reshape(last - first, WIN, D)
+
+    @pl.when(core == 0)
+    def _():
+        adjoint(0, 0, 2)
+        adjoint(1, 0, 1)
+
+    @pl.when(core == 1)
+    def _():
+        adjoint(0, 4, 5)
+        adjoint(1, 3, 5)
+
     for r in range(ROWS):
         rim_mid[r] = gext[core * 4 + r, 2 * WH:2 * WH + NJ * MID].astype(BF16)
     rim = Halo(rim_s, rim_r)
@@ -230,7 +258,23 @@
     for k in range(NJ):
         at = pl.ds(MID * k, MID)
         rims.append(rim.copy(k, rim_mid.at[:, at], far_mid.at[:, at], rim.far))
-    for c in rims[:2 + EARLY]:
+    for c in rims[2:2 + EARLY]:
+        c.start()
+
+    @pl.when(core == 0)
+    def _():
+        adjoint(0, 2, 5)
+        adjoint(1, 1, 5)
+
+    @pl.when(core == 1)
+    def _():
+        adjoint(0, 0, 4)
+        adjoint(1, 0, 3)
+
+    for r in range(6):
+        side_out[0, r] = gext[r, 0:WH].astype(BF16)
+        side_out[1, r] = pltpu.roll(gext[r, PAD:PAD + 32], 28, 0)[:WH].astype(BF16)
+    for c in rims[:2]:
         c.start()
 
     def core_send(p):
@@ -365,10 +409,10 @@
     z_send(1)
     z_sum(0)
     z_sum(1)
+    gathers = [gather_send(0)]
+    gathers.append(gather_send(1))
     for c in rims[2 + EARLY:-1]:
         c.start()
-    gathers = [gather_send(0)]
-    gathers.append(gather_send(1))
 
     for c in rims[2:]:
         c.wait_recv()
@@ -393,6 +437,20 @@
             mirrors.append(c)
     for c in mirrors:
         c.wait_recv()
+    for c in sends + corners + [share_w, share_e, pass_w, pass_e] + rims + core_copies + plane[0] + plane[1] + gathers[0][0] + gathers[1][0] + mirrors:
+        c.wait_send()
+    for p in range(2):
+        for k in range(1, 16):
+            @pl.when(owns(p, (z + k) % 16))
+            def _(p=p, k=k):
+                remote(z_out.at[p, 0], z_in.at[p, k], z_s.at[p, k], z_r.at[p, k], other).wait_send()
+
+            @pl.when(owns(p, z))
+            def _(p=p, k=k):
+                remote(z_all.at[p, 0], z_all.at[p, 0], zg_s.at[p, k], zg_r.at[p, k], other).wait_send()
+
+
+def unpack(total, out_in, gfield_in, out_ref, gfield_ref, gmix_ref, gin_ref, gout_ref):
     for n in range(3):
         gout_ref[:, 128 * n:128 * n + 128] = total[48 * n:48 * n + 48].reshape(HID, 128)
     for n in range(6):
@@ -400,38 +458,29 @@
     for b in range(K):
         folded = total[288 + 24 * b:312 + 24 * b].reshape(D, 128)
         gmix_ref[b] = folded[:, :DG].reshape(G, DG, DG)
-
-    for c in sends + corners + [pass_w, pass_e] + rims + core_copies + plane[0] + plane[1] + gathers[0][0] + gathers[1][0] + mirrors:
-        c.wait_send()
-    for p in range(2):
-        for k in range(1, 16):
-            @pl.when(owns(p, (z + k) % 16))
-            def _(p=p, k=k):
-                remote(z_out.at[p, 0], z_in.at[p, k], z_s.at[p, k], z_r.at[p, k], other).wait_send()
-
-            @pl.when(owns(p, z))
-            def _(p=p, k=k):
-                remote(z_all.at[p, 0], z_all.at[p, 0], zg_s.at[p, k], zg_r.at[p, k], other).wait_send()
+    out_ref[...] = jnp.swapaxes(out_in[...], 0, 1)
+    gfield_ref[...] = jnp.swapaxes(gfield_in[...], 0, 1)
 
 
 def body(field, row_shift, output_tile_index, tiles, mix, w_in, w_out, cotangent):
     vmem = pl.BlockSpec(memory_space=pltpu.VMEM)
     smem = pl.BlockSpec(memory_space=pltpu.SMEM)
+    anywhere = pl.BlockSpec(memory_space=pltpu.HBM)
     dma = pltpu.SemaphoreType.DMA
     v = pltpu.VMEM
-    return pl.pallas_call(
+    out, gfield, total = pl.pallas_call(
         kernel,
         name="block",
         out_shape=(
             jax.ShapeDtypeStruct((ROWS, LON, D), BF16),
             jax.ShapeDtypeStruct((ROWS, LON, D), BF16),
-            jax.ShapeDtypeStruct((K, G, DG, DG), BF16),
-            jax.ShapeDtypeStruct((D, HID), BF16),
-            jax.ShapeDtypeStruct((HID, D), BF16),
+            jax.ShapeDtypeStruct((TILES, 16, 128), BF16),
         ),
-        in_specs=[smem, smem] + [vmem] * 6,
-        out_specs=[vmem] * 5,
+        in_specs=[smem, smem, anywhere, anywhere, vmem, anywhere, anywhere, anywhere],
+        out_specs=[vmem] * 3,
         scratch_shapes=[
+            v((LON, ROWS, D), BF16), v((LON, ROWS, D), BF16), v((K, G, DG, DG), BF16), v((D, HID), BF16), v((HID, D), BF16),
+            dma((5,)),
             v((6, EXT, D), BF16), v((6, WH, D), BF16), v((2, WH, D), BF16), v((2, WH, D), BF16), v((WH, D), BF16), v((WH, D), BF16),
             v((ROWS, PAD, D), BF16),
             v((32, 128), F32), v((ROWS, K * JB, OFF * WIN), BF16), v((K * D, D), BF16), v((CELLS, K * D), BF16),
@@ -441,13 +490,27 @@
             v((WH, D), BF16), v((WH, D), BF16), v((2, PAD, D), BF16), v((2, PAD, D), BF16),
             v((2, 6, WH, D), BF16), v((2, 6, WH, D), BF16),
             v((TILES, 16, 128), BF16), v((2, HALF, 16, 128), BF16), v((2, HALF, 16, 128), BF16),
-            v((2, 16, PER, 16, 128), BF16), v((2, PER, 16, 128), F32), v((2, 16, 16, 128), F32),
-            v((2, PER, 16, 128), BF16), v((TILES, 16, 128), BF16),
+            v((2, 16, PER, 16, 128), BF16), v((2, PER, 16, 128), F32), v((2, 16, 16, 128), F32), v((2, PER, 16, 128), BF16),
             dma((13,)), dma((13,)), dma((13,)), dma((13,)), dma((2,)), dma((2,)),
         ] + [dma((2, 16))] * 10,
-        compiler_params=pltpu.CompilerParams(collective_id=0, has_side_effects=True, vmem_limit_bytes=48 * 2**20),
+        compiler_params=pltpu.CompilerParams(collective_id=0, has_side_effects=True, vmem_limit_bytes=60 * 2**20),
         cost_estimate=pl.CostEstimate(flops=4 * 10**9, bytes_accessed=8 * 10**6, transcendentals=3 * 10**5),
-    )(row_shift, output_tile_index, field, cotangent, tiles, mix, w_in, w_out)
+    )(row_shift, output_tile_index, jnp.swapaxes(field, 0, 1), jnp.swapaxes(cotangent, 0, 1), jnp.swapaxes(tiles, 1, 2), mix, w_in, w_out)
+    out, gfield, gmix, gin, gout = pl.pallas_call(
+        unpack,
+        name="unpack",
+        out_shape=(
+            jax.ShapeDtypeStruct((LON, ROWS, D), BF16),
+            jax.ShapeDtypeStruct((LON, ROWS, D), BF16),
+            jax.ShapeDtypeStruct((K, G, DG, DG), BF16),
+            jax.ShapeDtypeStruct((D, HID), BF16),
+            jax.ShapeDtypeStruct((HID, D), BF16),
+        ),
+        in_specs=[vmem] * 3,
+        out_specs=[vmem] * 5,
+        compiler_params=pltpu.CompilerParams(vmem_limit_bytes=60 * 2**20),
+    )(total, out, gfield)
+    return jnp.swapaxes(out, 0, 1), jnp.swapaxes(gfield, 0, 1), gmix, gin, gout
 
 
 def solution(mesh):

time: 123 us -> 118 us (0.959)
  the two profiles are of different devices: /device:TPU:1 before, /device:TPU:33 now
where the time goes in v3:
time: 118 us
  Pallas kernels  117 us (99%)
    pallas_call x1, Pallas kernels, body(): pl.pallas_call(kernel, name='block', out_shape=(jax.ShapeDtypeStruct((ROW...  114 us
    pallas_call x1, Pallas kernels, body(): pl.pallas_call(unpack, name='unpack', out_shape=(jax.ShapeDtypeStruct((LO...  3.1 us

profile of v3, /device:TPU:33, one launch (start us, length us, event | category | flops | bytes accessed | tf_op | source)
XLA Modules:
  0.0 117.6 jit_solution(14857101963242681788)
XLA Ops:
  0.6 113.8 %block.1 = (bf16[2,180,384]{2,1,0:T(8,128)(2,1)}, bf16[2,180,384]{2,1,0:T(8,128)(2,1)}, bf16[384,16,128]{2,1,0:T(8,128)(2,1)}) custom-call(s32[2]{0:T(128)} %shift_ref.1, s32[2]{0:T(128)} %index_ref.1, bf16[180,2,384]{2,1,0:T(2,128)(2,1)} %bitcast.5, bf16[180,2,384]{2,1,0:T(2,128)(2,1)} %bitcast.6, bf16[3,3,16,33]{3,2,1,0:T(8,128)(2,1)} %bitcast.9, ...), custom_call_target="tpu_custom_call" | custom-call | flops 4000000000 | bytes 8000000 | tf_op jit(solution)/shard_map/block/pallas_call | solution.py:471
  114.5 3.1 %unpack.1 = (bf16[180,2,384]{2,1,0:T(2,128)(2,1)}, bf16[180,2,384]{2,1,0:T(2,128)(2,1)}, bf16[3,4,96,96]{3,2,1,0:T(8,128)(2,1)}, bf16[384,768]{1,0:T(8,128)(2,1)}, bf16[768,384]{1,0:T(8,128)(2,1)}) custom-call(bf16[384,16,128]{2,1,0:T(8,128)(2,1)} %get-tuple-element.13.total, bf16[2,180,384]{2,1,0:T(8,128)(2,1)} %get-tuple-element.14.out_in, ...), custom_call_target="tpu_custom_call" | custom-call | tf_op jit(solution)/shard_map/unpack/pallas_call | solution.py:499

commit v4 on v3

--- a/solution.py
+++ b/solution.py
@@ -63,6 +63,7 @@
         self.far = ((lat + 64 - step) % 64, lon)
         west, east = (lon + 7) % 8, (lon + 1) % 8
         self.west, self.east = (lat, west), (lat, east)
+        self.near_west, self.near_east = (lat + step, west), (lat + step, east)
         self.sems_out, self.sems_in = sems_out, sems_in
 
     def copy(self, i, src, dst, to):
@@ -73,9 +74,9 @@
     shift_ref, index_ref, field_hbm, cot_hbm, tiles_ref, mix_hbm, win_hbm, wout_hbm,
     out_ref, gfield_ref, total,
     field_ref, cot_ref, mix_ref, win_ref, wout_ref, load_s,
-    ext, east_in, east_out, far_east, tail_out, tail_in, cot, taps, strip, mixd, basis, mixed, hidden, gpre, ghid, pre,
+    ext, east_in, east_out, far_east, tail_out, tail_in, begun, cot, taps, strip, mixd, basis, mixed, hidden, gpre, ghid, pre,
     gmixed, gbasis, gext, rim_mid, far_mid, rim_ends, far_ends, rim_tail, far_tail, rim_near_out, rim_near, side_out, side_in,
-    part, core_in, half_out, plane_in, z_out, z_in, z_all,
+    part, core_in, half_out, plane_in, z_out, z_half, z_in, z_all,
     halo_s, halo_r, rim_s, rim_r, core_s, core_r, plane_s, plane_r, z_s, z_r, zg_s, zg_r, pg_s, pg_r, cg_s, cg_r,
 ):
     x, y, z, core = position()
@@ -92,7 +93,7 @@
         return pz, device(x, y, pz, core)
 
     barrier = pltpu.get_barrier_semaphore()
-    greet = [halo.near, halo.far, halo.west, halo.east]
+    greet = [halo.near, halo.far, halo.west, halo.east, halo.near_west, halo.near_east]
     greet += [plane_peer(k)[1] for k in range(1, 16)] + [z_peer(k)[1] for k in range(1, 16)]
     for to in greet:
         pl.semaphore_signal(barrier, inc=1, device_id=to, device_id_type=MESH)
@@ -117,44 +118,6 @@
     tails = [ext[2 + r, 192:208].astype(F32) for r in range(ROWS)]
     tail_out[...] = (tails[0] + pltpu.roll(tails[1], 4, 0)).astype(BF16)
 
-    loads[1].wait()
-    cot[:, 0:LON] = jnp.swapaxes(cot_ref[...], 0, 1)
-    loads[2].wait()
-    ghid[...] = dot(cot[...].reshape(CELLS, D), wout_ref[...], ((1,), (1,)))
-    group = lambda n: (n >= DG).astype(jnp.int32) + (n >= 2 * DG).astype(jnp.int32) + (n >= 3 * DG).astype(jnp.int32)
-    row_i, col_i = (lax.broadcasted_iota(jnp.int32, (D, D), d) for d in (0, 1))
-    block = group(row_i) == group(col_i)
-    s_row, s_col = (lax.broadcasted_iota(jnp.int32, (DG, D), d) for d in (0, 1))
-    spread = (s_row == s_col - DG * group(s_col)).astype(BF16)
-    loads[3].wait()
-    for b in range(K):
-        wide = dot(mix_ref[b].reshape(D, DG), spread)
-        mixd[D * b:D * b + D] = jnp.where(block, wide, 0.0).astype(BF16)
-    taps[...] = jnp.zeros((32, 128), F32)
-    for r in range(ROWS):
-        s, t = shift_ref[r], index_ref[r]
-        for b in range(K):
-            chosen = lax.broadcasted_iota(jnp.int32, (16, WTAP), 0) == t
-            tile = [
-                jnp.sum(jnp.where(chosen, tiles_ref[b, k].astype(F32), 0.0), axis=0, keepdims=True) for k in range(K)]
-            for o in range(OFF):
-                line = jnp.zeros((1, WTAP), F32)
-                here = lat * ROWS + r + o - 2
-                inside = jnp.logical_and(here >= 0, here < NLAT)
-                for k in range(K):
-                    line = jnp.where(jnp.logical_and(inside, k == o - 1 - s), tile[k], line)
-                n = (r * K + b) * OFF + o
-                taps[n:n + 1, 0:WTAP] = line
-    for r in range(ROWS):
-        for b in range(K):
-            for o in range(OFF):
-                n = (r * K + b) * OFF + o
-                line = jnp.broadcast_to(taps[n:n + 1], (JB, WIN))
-                strip[r, JB * b:JB * b + JB, WIN * o:WIN * o + WIN] = pltpu.roll(
-                    line, 0, 1, stride=1, stride_axis=0).astype(BF16)
-
-    gext[...] = jnp.zeros((6, EXT, D), F32)
-    loads[4].wait()
     pl.semaphore_wait(barrier, len(greet))
 
     near_at = core * 4
@@ -172,16 +135,51 @@
     corners = [
         halo.copy(9, own_west, east_in.at[2:4], halo.west),
         halo.copy(10, east_out, ext.at[2:4, 0:16], halo.east),
+        halo.copy(11, own_west, east_in.at[pl.ds(near_at, 2)], halo.near_west),
+        halo.copy(12, east_out, ext.at[pl.ds(near_at, 2), 0:16], halo.near_east),
     ]
     for c in sends + [near] + corners:
         c.start()
 
-    corners[0].wait_recv()
-    share_w = halo.copy(11, east_in.at[2:4], east_in.at[pl.ds(near_at, 2)], halo.near)
-    share_w.start()
-    corners[1].wait_recv()
-    share_e = halo.copy(12, ext.at[2:4, 0:16], ext.at[pl.ds(near_at, 2), 0:16], halo.near)
-    share_e.start()
+    loads[1].wait()
+    cot[:, 0:LON] = jnp.swapaxes(cot_ref[...], 0, 1)
+    loads[2].wait()
+    ghid[...] = dot(cot[...].reshape(CELLS, D), wout_ref[...], ((1,), (1,)))
+    group = lambda n: (n >= DG).astype(jnp.int32) + (n >= 2 * DG).astype(jnp.int32) + (n >= 3 * DG).astype(jnp.int32)
+    row_i, col_i = (lax.broadcasted_iota(jnp.int32, (D, D), d) for d in (0, 1))
+    block = group(row_i) == group(col_i)
+    s_row, s_col = (lax.broadcasted_iota(jnp.int32, (DG, D), d) for d in (0, 1))
+    spread = (s_row == s_col - DG * group(s_col)).astype(BF16)
+    loads[3].wait()
+    for b in range(K):
+        wide = dot(mix_ref[b].reshape(D, DG), spread)
+        mixd[D * b:D * b + D] = jnp.where(block, wide, 0.0).astype(BF16)
+    taps[...] = jnp.zeros((32, 128), F32)
+    for r in range(ROWS):
+        s, t = shift_ref[r], index_ref[r]
+        for b in range(K):
+            chosen = lax.broadcasted_iota(jnp.int32, (16, WTAP), 0) == t
+            tile = [
+                jnp.sum(jnp.where(chosen, tiles_ref[b, k].astype(F32), 0.0), axis=0, keepdims=True) for k in range(K)]
+            for o in range(OFF):
+                line = jnp.zeros((1, WTAP), F32)
+                here = lat * ROWS + r + o - 2
+                inside = jnp.logical_and(here >= 0, here < NLAT)
+                for k in range(K):
+                    line = jnp.where(jnp.logical_and(inside, k == o - 1 - s), tile[k], line)
+                n = (r * K + b) * OFF + o
+                taps[n:n + 1, 0:WTAP] = line
+    for r in range(ROWS):
+        for b in range(K):
+            for o in range(OFF):
+                n = (r * K + b) * OFF + o
+                line = jnp.broadcast_to(taps[n:n + 1], (JB, WIN))
+                strip[r, JB * b:JB * b + JB, WIN * o:WIN * o + WIN] = pltpu.roll(
+                    line, 0, 1, stride=1, stride_axis=0).astype(BF16)
+
+    gext[...] = jnp.zeros((6, EXT, D), F32)
+    loads[4].wait()
+
     send_w.wait_recv()
     pass_w = halo.copy(7, ext.at[far_here, 16:32], east_in.at[far_here], halo.west)
     pass_w.start()
@@ -197,19 +195,41 @@
     pass_e = halo.copy(8, far_east, ext.at[far_here, 0:16], halo.east)
     pass_e.start()
 
-    near.wait()
-    for c in sends[3:] + [share_w, share_e, pass_w, pass_e]:
-        c.wait_recv()
-    for r in range(6):
+    def east_edge(r):
         edge = jnp.concatenate([east_in[r].astype(F32), jnp.zeros((WH, D), F32)], axis=0)
         ext[r, PAD:PAD + 32] = (ext[r, PAD:PAD + 32].astype(F32) + pltpu.roll(edge, 4, 0)).astype(BF16)
 
-    for r in range(ROWS):
-        for j in range(NJ):
-            window = ext[r:r + OFF, JB * j:JB * j + WIN].reshape(OFF * WIN, D)
-            found = dot(strip[r], window).astype(BF16)
-            for b in range(K):
-                basis[r * PAD + JB * j:r * PAD + JB * j + JB, D * b:D * b + D] = found[JB * b:JB * b + JB]
+    def filtered(r, j, first, last):
+        window = ext[r + first:r + last, JB * j:JB * j + WIN].reshape((last - first) * WIN, D)
+        return dot(strip[r, :, WIN * first:WIN * last], window)
+
+    near.wait()
+    for c in corners:
+        c.wait_recv()
+    for r in (2, 3):
+        east_edge(r)
+    for r in range(2):
+        east_edge(4 - core * 4 + r)
+    for c, ranges in ((0, ((2, 5), (1, 5))), (1, ((0, 4), (0, 3)))):
+        @pl.when(core == c)
+        def _(ranges=ranges):
+            for r in range(ROWS):
+                for j in range(NJ):
+                    begun[r * NJ + j] = filtered(r, j, *ranges[r])
+
+    for c in sends[3:] + [pass_w, pass_e]:
+        c.wait_recv()
+    for r in range(2):
+        east_edge(core * 4 + r)
+
+    for c, ranges in ((0, ((0, 2), (0, 1))), (1, ((4, 5), (3, 5)))):
+        @pl.when(core == c)
+        def _(ranges=ranges):
+            for r in range(ROWS):
+                for j in range(NJ):
+                    found = (begun[r * NJ + j] + filtered(r, j, *ranges[r])).astype(BF16)
+                    for b in range(K):
+                        basis[r * PAD + JB * j:r * PAD + JB * j + JB, D * b:D * b + D] = found[JB * b:JB * b + JB]
     own = ext[2:4, WH:WH + PAD].reshape(CELLS, D).astype(F32)
     mixed[...] = (own + dot(basis[...], mixd[...])).astype(BF16)
 
@@ -365,12 +385,13 @@
         for k in range(1, 16):
             acc += plane_in[p, k].astype(F32)
         z_out[p] = acc
+        z_half[p] = acc.astype(BF16)
         for k in range(1, 16):
             pz, to = z_peer(k)
 
             @pl.when(owns(p, pz))
             def _(k=k, pz=pz, to=to):
-                remote(z_out.at[p, tile_of(p, pz)], z_in.at[p, k], z_s.at[p, k], z_r.at[p, k], to).start()
+                remote(z_half.at[p, tile_of(p, pz)], z_in.at[p, k], z_s.at[p, k], z_r.at[p, k], to).start()
 
     def z_sum(p):
         tile = tile_of(p, z)
@@ -378,10 +399,10 @@
         @pl.when(owns(p, z))
         def _():
             for k in range(1, 16):
-                remote(z_out.at[p, 0], z_in.at[p, k], z_s.at[p, k], z_r.at[p, k], other).wait_recv()
+                remote(z_half.at[p, 0], z_in.at[p, k], z_s.at[p, k], z_r.at[p, k], other).wait_recv()
             acc = z_out[p, tile]
             for k in range(1, 16):
-                acc += z_in[p, k]
+                acc += z_in[p, k].astype(F32)
             z_all[p, tile] = acc.astype(BF16)
             for k in range(1, 16):
                 remote(z_all.at[p, tile], z_all.at[p, tile], zg_s.at[p, k], zg_r.at[p, k], z_peer(k)[1]).start()
@@ -409,10 +430,10 @@
     z_send(1)
     z_sum(0)
     z_sum(1)
+    for c in rims[2 + EARLY:-1]:
+        c.start()
     gathers = [gather_send(0)]
     gathers.append(gather_send(1))
-    for c in rims[2 + EARLY:-1]:
-        c.start()
 
     for c in rims[2:]:
         c.wait_recv()
@@ -437,13 +458,13 @@
             mirrors.append(c)
     for c in mirrors:
         c.wait_recv()
-    for c in sends + corners + [share_w, share_e, pass_w, pass_e] + rims + core_copies + plane[0] + plane[1] + gathers[0][0] + gathers[1][0] + mirrors:
+    for c in sends + corners + [pass_w, pass_e] + rims + core_copies + plane[0] + plane[1] + gathers[0][0] + gathers[1][0] + mirrors:
         c.wait_send()
     for p in range(2):
         for k in range(1, 16):
             @pl.when(owns(p, (z + k) % 16))
             def _(p=p, k=k):
-                remote(z_out.at[p, 0], z_in.at[p, k], z_s.at[p, k], z_r.at[p, k], other).wait_send()
+                remote(z_half.at[p, 0], z_in.at[p, k], z_s.at[p, k], z_r.at[p, k], other).wait_send()
 
             @pl.when(owns(p, z))
             def _(p=p, k=k):
@@ -468,6 +489,10 @@
     anywhere = pl.BlockSpec(memory_space=pltpu.HBM)
     dma = pltpu.SemaphoreType.DMA
     v = pltpu.VMEM
+    field, cotangent, tiles = (jnp.swapaxes(a, *axes) for a, axes in ((field, (0, 1)), (cotangent, (0, 1)), (tiles, (1, 2))))
+    row_shift, output_tile_index, field, cotangent, tiles, mix, w_in, w_out = (
+        pltpu.with_memory_space_constraint(a, pltpu.HBM)
+        for a in (row_shift, output_tile_index, field, cotangent, tiles, mix, w_in, w_out))
     out, gfield, total = pl.pallas_call(
         kernel,
         name="block",
@@ -482,7 +507,7 @@
             v((LON, ROWS, D), BF16), v((LON, ROWS, D), BF16), v((K, G, DG, DG), BF16), v((D, HID), BF16), v((HID, D), BF16),
             dma((5,)),
             v((6, EXT, D), BF16), v((6, WH, D), BF16), v((2, WH, D), BF16), v((2, WH, D), BF16), v((WH, D), BF16), v((WH, D), BF16),
-            v((ROWS, PAD, D), BF16),
+            v((ROWS * NJ, K * JB, D), F32), v((ROWS, PAD, D), BF16),
             v((32, 128), F32), v((ROWS, K * JB, OFF * WIN), BF16), v((K * D, D), BF16), v((CELLS, K * D), BF16),
             v((CELLS, D), BF16), v((CELLS, HID), BF16), v((CELLS, HID), BF16), v((CELLS, HID), F32), v((CELLS, 256), F32),
             v((CELLS, D), BF16), v((CELLS, K * D), BF16), v((6, EXT, D), F32),
@@ -490,12 +515,13 @@
             v((WH, D), BF16), v((WH, D), BF16), v((2, PAD, D), BF16), v((2, PAD, D), BF16),
             v((2, 6, WH, D), BF16), v((2, 6, WH, D), BF16),
             v((TILES, 16, 128), BF16), v((2, HALF, 16, 128), BF16), v((2, HALF, 16, 128), BF16),
-            v((2, 16, PER, 16, 128), BF16), v((2, PER, 16, 128), F32), v((2, 16, 16, 128), F32), v((2, PER, 16, 128), BF16),
+            v((2, 16, PER, 16, 128), BF16), v((2, PER, 16, 128), F32), v((2, PER, 16, 128), BF16),
+            v((2, 16, 16, 128), BF16), v((2, PER, 16, 128), BF16),
             dma((13,)), dma((13,)), dma((13,)), dma((13,)), dma((2,)), dma((2,)),
         ] + [dma((2, 16))] * 10,
-        compiler_params=pltpu.CompilerParams(collective_id=0, has_side_effects=True, vmem_limit_bytes=60 * 2**20),
+        compiler_params=pltpu.CompilerParams(collective_id=0, has_side_effects=True, vmem_limit_bytes=48 * 2**20),
         cost_estimate=pl.CostEstimate(flops=4 * 10**9, bytes_accessed=8 * 10**6, transcendentals=3 * 10**5),
-    )(row_shift, output_tile_index, jnp.swapaxes(field, 0, 1), jnp.swapaxes(cotangent, 0, 1), jnp.swapaxes(tiles, 1, 2), mix, w_in, w_out)
+    )(row_shift, output_tile_index, field, cotangent, tiles, mix, w_in, w_out)
     out, gfield, gmix, gin, gout = pl.pallas_call(
         unpack,
         name="unpack",
@@ -508,7 +534,7 @@
         ),
         in_specs=[vmem] * 3,
         out_specs=[vmem] * 5,
-        compiler_params=pltpu.CompilerParams(vmem_limit_bytes=60 * 2**20),
+        compiler_params=pltpu.CompilerParams(vmem_limit_bytes=48 * 2**20),
     )(total, out, gfield)
     return jnp.swapaxes(out, 0, 1), jnp.swapaxes(gfield, 0, 1), gmix, gin, gout
 

time: 118 us -> 112 us (0.949)
  the two profiles are of different devices: /device:TPU:33 before, /device:TPU:1 now
where the time goes in v4:
time: 112 us; the launch traced here: 111 us
  Pallas kernels  111 us (99%)
    pallas_call x1, Pallas kernels, body(): pl.pallas_call(kernel, name='block', out_shape=(jax.ShapeDtypeStruct((ROW...  109 us

profile of v4, /device:TPU:1, one launch (start us, length us, event | category | flops | bytes accessed | tf_op | source)
XLA Modules:
  0.0 111.3 jit_solution(14014700794312938303)
XLA Ops:
  0.6 109.1 %block.1 = (bf16[2,180,384]{2,1,0:T(8,128)(2,1)S(1)}, bf16[2,180,384]{2,1,0:T(8,128)(2,1)S(1)}, bf16[384,16,128]{2,1,0:T(8,128)(2,1)S(1)}) custom-call(s32[2]{0:T(128)} %shift_ref.1, s32[2]{0:T(128)} %index_ref.1, bf16[180,2,384]{2,1,0:T(2,128)(2,1)} %bitcast.5, bf16[180,2,384]{2,1,0:T(2,128)(2,1)} %bitcast.6, bf16[3,3,16,33]{3,2,1,0:T(8,128)(2,1)} %bitcast.9, ...), custom_call_target="tpu_custom_call" | custom-call | flops 4000000000 | bytes 8000000 | tf_op jit(solution)/shard_map/block/pallas_call | solution.py:496
  109.7 1.6 %unpack.1 = (bf16[180,2,384]{2,1,0:T(2,128)(2,1)}, bf16[180,2,384]{2,1,0:T(2,128)(2,1)}, bf16[3,4,96,96]{3,2,1,0:T(8,128)(2,1)}, bf16[384,768]{1,0:T(8,128)(2,1)}, bf16[768,384]{1,0:T(8,128)(2,1)}) custom-call(bf16[384,16,128]{2,1,0:T(8,128)(2,1)S(1)} %get-tuple-element.13.total, bf16[2,180,384]{2,1,0:T(8,128)(2,1)S(1)} %get-tuple-element.14.out_in, ...), custom_call_target="tpu_custom_call" | custom-call | tf_op jit(solution)/shard_map/unpack/pallas_call | solution.py:525

commit v5 on v4

--- a/solution.py
+++ b/solution.py
@@ -435,6 +435,15 @@
     gathers = [gather_send(0)]
     gathers.append(gather_send(1))
 
+    mirrors = gathers[0][1] + gathers[1][1]
+    for p in range(2):
+        for k in range(1, 16):
+            gathers[p][0][k - 1].wait_recv()
+            qx, qy = (x + 4 - k // 4) % 4, (y + 4 - k % 4) % 4
+            at = pl.ds(PIECE * p + HALF * core + PER * (qx * 4 + qy), PER)
+            c = remote(total.at[at], total.at[at], cg_s.at[p, k], cg_r.at[p, k], other)
+            c.start()
+            mirrors.append(c)
     for c in rims[2:]:
         c.wait_recv()
     gm = gmixed[...].reshape(ROWS, PAD, D).astype(F32)
@@ -447,15 +456,6 @@
         gext[2 + r, 192:208] += tail if r == 0 else pltpu.roll(tail, 12, 0)
         gfield_ref[r] = gext[2 + r, WH:WH + LON].astype(BF16)
 
-    mirrors = gathers[0][1] + gathers[1][1]
-    for p in range(2):
-        for k in range(1, 16):
-            gathers[p][0][k - 1].wait_recv()
-            qx, qy = (x + 4 - k // 4) % 4, (y + 4 - k % 4) % 4
-            at = pl.ds(PIECE * p + HALF * core + PER * (qx * 4 + qy), PER)
-            c = remote(total.at[at], total.at[at], cg_s.at[p, k], cg_r.at[p, k], other)
-            c.start()
-            mirrors.append(c)
     for c in mirrors:
         c.wait_recv()
     for c in sends + corners + [pass_w, pass_e] + rims + core_copies + plane[0] + plane[1] + gathers[0][0] + gathers[1][0] + mirrors:

time: 112 us -> 112 us (level)
  no operation moved by 1% of the time
where the time goes in v5:
time: 112 us; the launch traced here: 111 us
  Pallas kernels  111 us (99%)
    pallas_call x1, Pallas kernels, body(): pl.pallas_call(kernel, name='block', out_shape=(jax.ShapeDtypeStruct((ROW...  109 us

profile of v5, /device:TPU:1, one launch (start us, length us, event | category | flops | bytes accessed | tf_op | source)
XLA Modules:
  0.0 111.3 jit_solution(12935010607888428863)
XLA Ops:
  0.6 109.1 %block.1 = (bf16[2,180,384]{2,1,0:T(8,128)(2,1)S(1)}, bf16[2,180,384]{2,1,0:T(8,128)(2,1)S(1)}, bf16[384,16,128]{2,1,0:T(8,128)(2,1)S(1)}) custom-call(s32[2]{0:T(128)} %shift_ref.1, s32[2]{0:T(128)} %index_ref.1, bf16[180,2,384]{2,1,0:T(2,128)(2,1)} %bitcast.5, bf16[180,2,384]{2,1,0:T(2,128)(2,1)} %bitcast.6, bf16[3,3,16,33]{3,2,1,0:T(8,128)(2,1)} %bitcast.9, ...), custom_call_target="tpu_custom_call" | custom-call | flops 4000000000 | bytes 8000000 | tf_op jit(solution)/shard_map/block/pallas_call | solution.py:496
  109.7 1.6 %unpack.1 = (bf16[180,2,384]{2,1,0:T(2,128)(2,1)}, bf16[180,2,384]{2,1,0:T(2,128)(2,1)}, bf16[3,4,96,96]{3,2,1,0:T(8,128)(2,1)}, bf16[384,768]{1,0:T(8,128)(2,1)}, bf16[768,384]{1,0:T(8,128)(2,1)}) custom-call(bf16[384,16,128]{2,1,0:T(8,128)(2,1)S(1)} %get-tuple-element.13.total, bf16[2,180,384]{2,1,0:T(8,128)(2,1)S(1)} %get-tuple-element.14.out_in, ...), custom_call_target="tpu_custom_call" | custom-call | tf_op jit(solution)/shard_map/unpack/pallas_call | solution.py:525
